TPU v7x, 32 devices: a whole 2x2x4 slice. The times are simulated.
32 devices in a mesh: seq: 8 (over z, x), tensor: 4 (over y, core).
Axes of the slice: x: 2, y: 2, z: 4, core: 2. Of those that a mesh axis runs over, the one named last changes fastest.
Arguments:
- queries: bfloat16 [2560, 2048], P('seq', 'tensor'), may hold values from -8 to 8
- key_rows: bfloat16 [2560, 512], P('seq', 'tensor'), may hold values from -8 to 8
- value_rows: bfloat16 [2560, 512], P('seq', 'tensor'), may hold values from -6 to 6
- out_weight: bfloat16 [2048, 8192], P('tensor', 'seq'), may hold values from -0.125 to 0.125
- residual_in: bfloat16 [2560, 8192], P('seq'), may hold values from -0.1796875 to 0.1796875
- norm_gain: bfloat16 [8192], replicated, may hold values from 0.099609375 to 1.8984375
- prompt_lengths: int32 [18], replicated, may hold values from 1 to 1280, 2560 in all
Outputs:
- normed: bfloat16 [2560, 8192], P('seq')
- cache_keys: bfloat16 [5632, 512], P('seq', 'tensor')
- cache_values: bfloat16 [5632, 512], P('seq', 'tensor')
Inputs may be any that keep to these rules, and one draw needn't show every extreme that they name: `prompt_lengths`: the 18 lengths sum to 2560, and the largest is 1280.
All inputs are finite; a program needn't handle non-finite values.
Results may differ from a plain program's by a relative error of at most 0.019.
Values may be sent and summed in bfloat16 or wider, within the bound.
A program may use at most 192 MiB of HBM per device.

v0:
```python
import math

import jax
import jax.numpy as jnp
from jax import lax
from jax.sharding import PartitionSpec as P

HD = 128
PAGE = 128
SLOT_DEV = 704


def position_of(stored, per_device, devices):
    half_block = per_device // 2
    device = stored // per_device
    offset = stored % per_device
    return jnp.where(
        offset < half_block,
        device * half_block + offset,
        (2 * devices - 1 - device) * half_block + offset - half_block,
    )


def stored_row(position, per_device, devices):
    half_block = per_device // 2
    block_index = position // half_block
    device = jnp.where(block_index < devices, block_index, 2 * devices - 1 - block_index)
    offset = position % half_block + jnp.where(block_index < devices, 0, half_block)
    return device * per_device + offset


def segment_of(position, lengths):
    doc_ends = jnp.cumsum(lengths, dtype=jnp.int32)
    return jnp.sum(
        (position[:, None] >= doc_ends[None, :]).astype(jnp.int32), axis=1, dtype=jnp.int32
    )


def slot_source(slot_ids, lengths, page_size):
    padded = (lengths + page_size - 1) // page_size * page_size
    page_ends = jnp.cumsum(padded, dtype=jnp.int32)
    page_starts = page_ends - padded
    doc_ends = jnp.cumsum(lengths, dtype=jnp.int32)
    doc_starts = doc_ends - lengths
    prompt = jnp.sum(
        (slot_ids[:, None] >= page_ends[None, :]).astype(jnp.int32), axis=1, dtype=jnp.int32
    )
    clipped = jnp.minimum(prompt, lengths.shape[0] - 1)
    within = slot_ids - jnp.take(page_starts, clipped)
    is_live = (prompt < lengths.shape[0]) & (within < jnp.take(lengths, clipped))
    return (jnp.take(doc_starts, clipped) + within, is_live)


def body(queries, key_rows, value_rows, out_weight, residual_in, norm_gain, prompt_lengths):
    seq_count = lax.axis_size("seq")
    seq_index = lax.axis_index("seq")
    per_device = queries.shape[0]
    kv_local = key_rows.shape[1] // HD
    group_size = queries.shape[1] // (kv_local * HD)
    score_scale = 1.0 / math.sqrt(HD)
    local_rows = jnp.arange(per_device, dtype=jnp.int32) + seq_index * per_device
    my_position = position_of(local_rows, per_device, seq_count)
    my_segment = segment_of(my_position, prompt_lengths)
    grouped = queries.reshape(per_device, kv_local, group_size, HD)
    key_piece = lax.all_gather(key_rows, "seq", axis=0, tiled=True)
    value_piece = lax.all_gather(value_rows, "seq", axis=0, tiled=True)
    piece_rows = key_piece.shape[0]
    key_position = position_of(jnp.arange(piece_rows, dtype=jnp.int32), per_device, seq_count)
    key_segment = segment_of(key_position, prompt_lengths)
    allowed = (key_position[None, :] <= my_position[:, None]) & (
        key_segment[None, :] == my_segment[:, None]
    )
    top_old = jnp.full((kv_local, group_size, per_device), -1e30, jnp.float32)
    scores = (
        jnp.einsum(
            "qgjd,kgd->gjqk",
            grouped,
            key_piece.reshape(piece_rows, kv_local, HD),
            preferred_element_type=jnp.float32,
        )
        * score_scale
    )
    scores = jnp.where(allowed, scores, -1e30)
    top_new = jnp.maximum(top_old, jnp.max(scores, axis=-1))
    weights = jnp.where(allowed, jnp.exp(scores - top_new[..., None]), 0.0)
    total_new = jnp.sum(weights, axis=-1)
    accum_new = jnp.einsum(
        "gjqk,kgd->gjqd",
        weights.astype(jnp.bfloat16),
        value_piece.reshape(piece_rows, kv_local, HD),
        preferred_element_type=jnp.float32,
    )
    attended = jnp.transpose(accum_new / total_new[..., None], (2, 0, 1, 3))
    attended = attended.reshape(per_device, -1).astype(jnp.bfloat16)
    partial_value = jnp.dot(
        attended,
        lax.all_gather(out_weight, "seq", axis=1, tiled=True),
        preferred_element_type=jnp.float32,
    )
    projected = lax.psum(partial_value.astype(jnp.bfloat16), "tensor").astype(jnp.float32)
    hidden = residual_in.astype(jnp.float32) + projected
    mean_square = jnp.mean(hidden * hidden, axis=-1, keepdims=True)
    normed = (hidden * lax.rsqrt(mean_square + 1e-05) * norm_gain.astype(jnp.float32)).astype(
        jnp.bfloat16
    )
    slot_ids = seq_index * SLOT_DEV + jnp.arange(SLOT_DEV, dtype=jnp.int32)
    source, is_live = slot_source(slot_ids, prompt_lengths, PAGE)
    target = stored_row(source, per_device, seq_count)
    empty_cache = jnp.zeros((SLOT_DEV, kv_local * HD), jnp.bfloat16)
    key_piece = lax.all_gather(key_rows, "seq", axis=0, tiled=True)
    value_piece = lax.all_gather(value_rows, "seq", axis=0, tiled=True)
    piece_rows = key_piece.shape[0]
    found = is_live & (target >= 0) & (target < piece_rows)
    safe_index = jnp.clip(target, 0, piece_rows - 1)
    cache_keys = jnp.where(found[:, None], jnp.take(key_piece, safe_index, axis=0), empty_cache)
    cache_values = jnp.where(found[:, None], jnp.take(value_piece, safe_index, axis=0), empty_cache)
    return (normed, cache_keys, cache_values)


def solution(mesh):
    return jax.shard_map(
        body,
        mesh=mesh,
        in_specs=(
            P("seq", "tensor"),
            P("seq", "tensor"),
            P("seq", "tensor"),
            P("tensor", "seq"),
            P("seq", None),
            P(),
            P(),
        ),
        out_specs=(P("seq", None), P("seq", "tensor"), P("seq", "tensor")),
        check_vma=False,
    )
```

profile of v0, /device:TPU:0, one launch (start us, length us, event | category | flops | bytes accessed | tf_op | source)
XLA Modules:
  0.0 276.5 jit_solution(14950965900229712064)
XLA Ops:
  7.2 0.0 copy-start
  7.2 0.0 all-gather.2.cloned.1.call-start
  7.2 0.7 all-gather.2.cloned.1.call-update
  7.9 0.0 all-reduce.2.cloned.1.call-start
  8.0 0.7 copy.17
  8.7 0.1 reduce.2
  8.9 0.1 convert_reduce_fusion.2
  9.0 0.1 convert_reduce_fusion
  9.1 35.4 %all_gather.11 = bf16[2560,128]{1,0:T(8,128)(2,1)S(1)} all-gather(bf16[320,128]{1,0:T(8,128)(2,1)} %param.12), channel_id=1, replica_groups=mesh['seq'=8,'tensor'=4] {'seq'}, dimensions={0}, use_global_device_ids=true | all-gather | bytes 737280 | tf_op jit(solution)/shard_map/all_gather | solution.py:65
  44.5 0.8 compare_and_fusion
  45.3 0.0 copy-done
  45.3 0.0 copy-start.3
  45.3 6.3 %fusion = (f32[4,320]{1,0:T(4,128)S(1)}, f32[2560,320,4]{0,1,2:T(8,128)}) fusion(pred[320,2560]{1,0:T(8,128)(4,1)S(1)} %compare_and_fusion, bf16[2560,128]{1,0:T(8,128)(2,1)S(1)} %all_gather.11, bf16[320,512]{1,0:T(8,128)(2,1)S(1)} %copy-done), kind=kOutput, calls=%fused_computation.4 | convolution fusion | flops 848689920 | bytes 14914560 | tf_op jit(solution)/shard_map/qgjd,kgd->gjqk/dot_general | solution.py:75
  51.6 0.0 copy-done.3
  51.6 33.4 %all_gather.12 = bf16[2560,128]{1,0:T(8,128)(2,1)S(1)} all-gather(bf16[320,128]{1,0:T(8,128)(2,1)S(1)} %copy-done.3), channel_id=1, replica_groups=mesh['seq'=8,'tensor'=4] {'seq'}, dimensions={0}, use_global_device_ids=true | all-gather | bytes 737280 | tf_op jit(solution)/shard_map/all_gather | solution.py:66
  85.1 8.9 %fusion.1 = f32[4,320]{1,0:T(4,128)S(1)} fusion(f32[2560,320,4]{0,1,2:T(8,128)} %get-tuple-element.66, f32[4,320]{1,0:T(4,128)S(1)} %broadcast_maximum_fusion, pred[320,2560]{1,0:T(8,128)(4,1)S(1)} %compare_and_fusion), kind=kLoop, calls=%fused_computation.9 | loop fusion | flops 16382720 | bytes 13936640 | tf_op jit(solution)/shard_map/reduce_sum | solution.py:86
  94.0 7.0 %fusion.13 = bf16[320,1,4,128]{3,0,2,1:T(8,128)(2,1)S(1)} fusion(f32[2560,320,4]{0,1,2:T(8,128)} %get-tuple-element.66, f32[4,320]{1,0:T(4,128)S(1)} %broadcast_maximum_fusion, pred[320,2560]{1,0:T(8,128)(4,1)S(1)} %compare_and_fusion, bf16[2560,128]{1,0:T(8,128)(2,1)S(1)} %all_gather.12, f32[4,320]{1,0:T(4,128)S(1)} %fusion.1), kind=kOutput, calls=%fused_computation.17 | convolution fusion | flops 855572480 | bytes 14919680 | tf_op jit(solution)/shard_map/gjqk,kgd->gjqd/dot_general | solution.py:87
  101.0 0.3 copy.19
  101.2 0.0 copy-start.2
  101.2 45.1 %all-gather.2.cloned.1.call-done = bf16[512,8192]{1,0:T(8,128)(2,1)} async-done(((bf16[512,1024]{1,0:T(8,128)(2,1)}), bf16[512,8192]{1,0:T(8,128)(2,1)}) %all-gather.2.cloned.1.call-update) | async-done | bytes 8388624 | tf_op jit(solution)/shard_map/all_gather | solution.py:97
  146.4 0.0 copy-start.4
  146.4 8.0 %convolution_convert_fusion = bf16[320,8192]{1,0:T(8,128)(2,1)} fusion(bf16[512,8192]{1,0:T(8,128)(2,1)} %all-gather.2.cloned.1.call-done, bf16[40,8,4,128]{3,2,1,0:T(4,128)(2,1)S(1)} %bitcast.114), kind=kOutput, calls=%fused_computation.5 | convolution fusion | flops 2686976000 | bytes 13959168 | tf_op jit(solution)/shard_map/dot_general | solution.py:95
  154.3 0.0 all-reduce.2.cloned.1.call-update
  154.4 0.0 copy-done.2
  154.4 0.1 copy.20
  154.5 0.1 reduce.3
  154.7 0.7 fusion.52
  155.4 0.7 fusion.51
  156.1 0.7 fusion.49
  156.9 0.1 convert_reduce_fusion.1
  157.0 33.8 %compare_and_fusion.3 = (pred[704]{0:T(1024)(128)(4,1)S(1)}, s32[704]{0:T(1024)S(1)}) fusion(s32[704]{0:T(1024)S(1)} %convert_reduce_fusion.1, s32[]{:T(128)} %bitcast.44, s32[]{:T(128)} %bitcast.43, s32[]{:T(128)} %bitcast.42, s32[]{:T(128)} %bitcast.41, s32[]{:T(128)} %bitcast.40, s32[]{:T(128)} %bitcast.39, s32[]{:T(128)} %bitcast.38, s32[]{:T(128)} %bitcast.37, ...), kind=kLoop, calls=%fused_computation.64 | loop fusion | flops 75328 | bytes 6556 | tf_op jit(solution)/shard_map/and | solution.py:113
  190.8 2.0 gather_fusion
  192.8 2.0 gather_fusion.1
  194.8 0.0 copy-done.4
  194.9 1.0 select_select_fusion
  195.9 60.7 %all-reduce.2.cloned.1.call-done = bf16[320,8192]{1,0:T(8,128)(2,1)} async-done(((bf16[320,8192]{1,0:T(8,128)(2,1)}), bf16[320,8192]{1,0:T(8,128)(2,1)}) %all-reduce.2.cloned.1.call-update) | async-done | bytes 5242896 | tf_op jit(solution)/shard_map/psum | solution.py:100
  256.5 0.0 copy-start.1
  256.5 6.0 %multiply_reduce_fusion = f32[320]{0:T(512)S(1)} fusion(bf16[320,8192]{1,0:T(8,128)(2,1)} %all-reduce.2.cloned.1.call-done, bf16[320,8192]{1,0:T(8,128)(2,1)} %param.15), kind=kLoop, calls=%fused_computation.7 | loop fusion | flops 13106880 | bytes 10487040 | tf_op jit(solution)/shard_map/reduce_sum | solution.py:102
  262.5 0.0 copy-done.1
  262.5 7.1 %multiply_convert_fusion = bf16[320,8192]{1,0:T(8,128)(2,1)} fusion(bf16[320,8192]{1,0:T(8,128)(2,1)S(1)} %copy-done.1, bf16[320,8192]{1,0:T(8,128)(2,1)} %param.15, f32[8192]{0:T(1024)S(1)} %convert_element_type.49, f32[320]{0:T(512)S(1)} %add_rsqrt_fusion), kind=kLoop, calls=%fused_computation.6 | loop fusion | flops 15728640 | bytes 15762688 | tf_op jit(solution)/shard_map/convert_element_type | solution.py:103
  (13 shorter events, 0.2 us)
Async XLA Ops:
  7.2 38.1 %copy-start = (bf16[320,512]{1,0:T(8,128)(2,1)S(1)}, bf16[320,512]{1,0:T(8,128)(2,1)}, u32[]{:S(2)}) copy-start(bf16[320,512]{1,0:T(8,128)(2,1)} %param.11) | copy-start | bytes 983044
  7.2 139.2 %all-gather.2.cloned.1.call-start = ((), (), s32[]{:S(2)}) async-start(), calls=%async_computation | async-start | bytes 9437184 | tf_op jit(solution)/shard_map/all_gather | solution.py:97
  7.9 248.6 %all-reduce.2.cloned.1.call-start = ((), (), s32[]{:S(2)}) async-start(), calls=%async_computation.1 | async-start | bytes 10485760 | tf_op jit(solution)/shard_map/psum | solution.py:100
  45.3 6.3 %copy-start.3 = (bf16[320,128]{1,0:T(8,128)(2,1)S(1)}, bf16[320,128]{1,0:T(8,128)(2,1)}, u32[]{:S(2)}) copy-start(bf16[320,128]{1,0:T(8,128)(2,1)} %param.13) | copy-start | bytes 245764
  101.2 53.1 %copy-start.2 = (s32[18]{0:T(128)S(1)}, s32[18]{0:T(128)}, u32[]{:S(2)}) copy-start(s32[18]{0:T(128)} %param.17) | copy-start | bytes 220
  146.4 48.5 %copy-start.4 = (bf16[8192]{0:T(1024)(128)(2,1)S(1)}, bf16[8192]{0:T(1024)(128)(2,1)}, u32[]{:S(2)}) copy-start(bf16[8192]{0:T(1024)(128)(2,1)} %param.16) | copy-start | bytes 49156
  256.5 6.0 %copy-start.1 = (bf16[320,8192]{1,0:T(8,128)(2,1)S(1)}, bf16[320,8192]{1,0:T(8,128)(2,1)}, u32[]{:S(2)}) copy-start(bf16[320,8192]{1,0:T(8,128)(2,1)} %all-reduce.2.cloned.1.call-done) | copy-start | bytes 15728644
Sparse Core Ops, SparseCore 0:
  10.2 136.1 all-gather.1
  154.5 101.9 all-reduce.1
where the time goes:
time: 277 us; the launch traced here: 276 us
  waiting for transfers between devices  106 us (38%)
  blocking collectives  68.8 us (25%)
  other arithmetic  58.2 us (21%)
  matrix products  21.3 us (8%)
  between operations  14.2 us (5%)
  local copies, waits for them, and re-layouts  7.37 us (3%)
    psum x1, waiting for transfers between devices, body(): lax.psum(partial_value.astype(jnp.bfloat16), 'tensor').astype(jnp.float32)  60.7 us
    all_gather x1, waiting for transfers between devices, body(): lax.all_gather(out_weight, 'seq', axis=1, tiled=True)  45.1 us
    all_gather x1, blocking collectives, body(): key_piece = lax.all_gather(key_rows, 'seq', axis=0, tiled=True)  35.4 us
    and x1, other arithmetic, body(): found = is_live & (target >= 0) & (target < piece_rows)  33.8 us
    all_gather x1, blocking collectives, body(): value_piece = lax.all_gather(value_rows, 'seq', axis=0, tiled=True)  33.4 us
    reduce_sum x1, other arithmetic, body(): total_new = jnp.sum(weights, axis=-1)  8.9 us
    dot_general x1, matrix products, body(): jnp.dot(attended, lax.all_gather(out_weight, 'seq', axis=1, tiled=True),...  7.99 us
    convert_element_type x1, other arithmetic, body(): (hidden * lax.rsqrt(mean_square + 1e-05) * norm_gain.astype(jnp.float32))...  7.13 us
  transfers between devices with their start and end apart: 2, of which 2 were waited for; matrix products, arithmetic and copies ran while one was open for 24% of the time, Pallas kernels for 0%

commit v1 on v0

v1 whole, which is shorter than its diff:
```python
import functools
import math

import jax
import jax.numpy as jnp
from jax import lax
from jax.experimental import pallas as pl
from jax.experimental.pallas import tpu as pltpu
from jax.sharding import PartitionSpec as P

HD = 128
PAGE = 128
SLOT_DEV = 704
LINE = 4
CORES = 2
KEYS = 256
ROW_TILE = 16
MESH = pl.DeviceIdType.MESH


def kernel(
    n_seq,
    n_tensor,
    q_ref,
    k_ref,
    v_ref,
    w_ref,
    res_ref,
    gain_ref,
    len_ref,
    normed_ref,
    ck_ref,
    cv_ref,
    kv,
    wbuf,
    att,
    prod,
    proj,
    res,
    m_ref,
    l_ref,
    acc_ref,
    kv_send,
    kv_recv,
    w_send,
    w_recv,
    w_local,
    a_send,
    a_recv,
    p_send,
    p_recv,
    res_sem,
):
    rest = n_seq // LINE
    pairs = n_tensor // CORES
    rows = q_ref.shape[0]
    half = rows // 2
    tokens = kv.shape[0]
    heads = q_ref.shape[1] // HD
    depth = w_ref.shape[0]
    width = wbuf.shape[2]
    parts = w_ref.shape[1] // width
    n_prompts = len_ref.shape[0]

    seq = lax.axis_index("seq")
    ten = lax.axis_index("tensor")
    line = seq // rest
    col = seq % rest
    pair = ten // CORES
    core = ten % CORES

    def line_peer(j):
        return ((line + j) % LINE) * rest + col

    def col_peer(i):
        return line * rest + (col + i) % rest

    def pair_peer(i):
        return ((pair + i) % pairs) * CORES + core

    twin = pair * CORES + 1 - core

    def remote(src, dst, send, recv, to_seq, to_ten):
        return pltpu.make_async_remote_copy(
            src_ref=src,
            dst_ref=dst,
            send_sem=send,
            recv_sem=recv,
            device_id=(to_seq, to_ten),
            device_id_type=MESH,
        )

    res_copy = pltpu.make_async_copy(res_ref, res, res_sem)
    res_copy.start()

    barrier = pltpu.get_barrier_semaphore()
    greeted = 0
    for j in range(1, LINE):
        pl.semaphore_signal(barrier, inc=1, device_id=(line_peer(j), ten), device_id_type=MESH)
        greeted += 1
    for i in range(rest):
        for k in range(n_tensor):
            if i == 0 and k == 0:
                continue
            pl.semaphore_signal(
                barrier,
                inc=1,
                device_id=(col_peer(i), (ten + k) % n_tensor),
                device_id_type=MESH,
            )
            greeted += 1

    def kv_rows(source, h):
        block = source if h == 0 else 2 * n_seq - 1 - source
        return pl.ds(pl.multiple_of(block * half, half), half)

    for h in range(2):
        kv[kv_rows(seq, h), :HD] = k_ref[h * half : (h + 1) * half, :]
        kv[kv_rows(seq, h), HD:] = v_ref[h * half : (h + 1) * half, :]
    pl.semaphore_wait(barrier, greeted)

    sent = []

    def kv_copy(source, h, j, i, to_seq):
        at = kv.at[kv_rows(source, h)]
        return remote(at, at, kv_send.at[j, i, h], kv_recv.at[source, h], to_seq, ten)

    def kv_start(source, h, j, i, to_seq):
        copy = kv_copy(source, h, j, i, to_seq)
        copy.start()
        sent.append(copy)

    for h in range(2):
        for j in (2, 1, 3):
            kv_start(seq, h, j, 0, line_peer(j))
    for h in range(2):
        for i in range(1, rest):
            kv_start(seq, h, 0, i, col_peer(i))
    for j in (1, 3, 2):
        source = line_peer(j)
        for h in range(2):
            kv_copy(source, h, j, 0, seq).wait_recv()
            for i in range(1, rest):
                kv_start(source, h, j, i, col_peer(i))

    mine = (col * parts <= ten) & (ten < (col + 1) * parts)
    for i in range(rest):
        for k in range(parts):
            target = col * parts + k
            piece = w_ref.at[:, pl.ds(k * width, width)]
            copy = remote(
                piece, wbuf.at[ten], w_send.at[i, k], w_recv.at[ten], col_peer(i), target
            )
            if i == 0:

                @pl.when(target != ten)
                def _(copy=copy):
                    copy.start()

                @pl.when(target == ten)
                def _(piece=piece):
                    pltpu.make_async_copy(piece, wbuf.at[ten], w_local).start()

            else:
                copy.start()

    starts = [jnp.int32(0)]
    for p in range(n_prompts - 1):
        starts.append(starts[-1] + len_ref[p])

    for i in range(1, rest):
        for j in range(LINE):
            source = ((line + j) % LINE) * rest + (col + i) % rest
            for h in range(2):
                kv_copy(source, h, j, i, seq).wait_recv()

    scale = 1.0 / math.sqrt(HD)
    for h in range(2):
        block = seq if h == 0 else 2 * n_seq - 1 - seq
        query = jnp.concatenate(
            [q_ref[h * half : (h + 1) * half, g * HD : (g + 1) * HD] for g in range(heads)], axis=0
        )
        position = block * half + lax.broadcasted_iota(jnp.int32, (half, 1), 0)
        begin = jnp.zeros((half, 1), jnp.int32)
        for p in range(1, n_prompts):
            begin = jnp.where(starts[p] <= position, starts[p], begin)
        m_ref[...] = jnp.full_like(m_ref, -1e20)
        l_ref[...] = jnp.zeros_like(l_ref)
        acc_ref[...] = jnp.zeros_like(acc_ref)

        def step(c, carry, query=query, position=position, begin=begin):
            at = pl.ds(pl.multiple_of(c * KEYS, KEYS), KEYS)
            scores = lax.dot_general(
                query,
                kv[at, :HD],
                (((1,), (1,)), ((), ())),
                preferred_element_type=jnp.float32,
            )
            where = c * KEYS + lax.broadcasted_iota(jnp.int32, (half, KEYS), 1)
            bias = jnp.where((where >= begin) & (where <= position), 0.0, -1e30)
            scores = scores * scale + jnp.concatenate([bias] * heads, axis=0)
            old = m_ref[:, :1]
            top = jnp.maximum(old, jnp.max(scores, axis=1, keepdims=True))
            shrink = jnp.exp(old - top)
            weights = jnp.exp(scores - top)
            total = l_ref[:, :1] * shrink + jnp.sum(weights, axis=1, keepdims=True)
            acc_ref[...] = acc_ref[...] * shrink + jnp.dot(
                weights.astype(jnp.bfloat16), kv[at, HD:], preferred_element_type=jnp.float32
            )
            m_ref[...] = jnp.broadcast_to(top, m_ref.shape)
            l_ref[...] = jnp.broadcast_to(total, l_ref.shape)
            return carry

        lax.fori_loop(0, ((block + 1) * half + KEYS - 1) // KEYS, step, 0)
        result = (acc_ref[...] / l_ref[...]).astype(jnp.bfloat16)
        for g in range(heads):
            att[line, ten, h * half : (h + 1) * half, g * HD : (g + 1) * HD] = result[
                g * half : (g + 1) * half
            ]

    def piece_copy(buf, send, recv, at_line, at_ten, slot, to_ten):
        at = buf.at[at_line, at_ten]
        return remote(at, at, send.at[slot], recv.at[at_line, at_ten], seq, to_ten)

    def spread(buf, send, recv, j):
        at_line = (line + j) % LINE
        for i in range(1, pairs):
            copy = piece_copy(buf, send, recv, at_line, ten, (j, i), pair_peer(i))
            copy.start()
            sent.append(copy)
        copy = piece_copy(buf, send, recv, at_line, ten, (j, pairs), twin)
        copy.start()
        sent.append(copy)

    def relay(buf, send, recv, j):
        at_line = (line + j) % LINE
        for i in range(1, pairs):
            source = pair_peer(pairs - i)
            piece_copy(buf, send, recv, at_line, source, (j, 0), ten).wait_recv()
            copy = piece_copy(buf, send, recv, at_line, source, (j, pairs + i), twin)
            copy.start()
            sent.append(copy)

    def settle(buf, send, recv, j):
        at_line = (line + j) % LINE
        for y in range(pairs):
            source = y * CORES + 1 - core
            piece_copy(buf, send, recv, at_line, source, (j, 0), ten).wait_recv()

    def arrive(buf, send, recv, j):
        at_line = (line + j) % LINE
        piece_copy(buf, send, recv, at_line, ten, (j, 0), ten).wait_recv()
        spread(buf, send, recv, j)

    for j in (2, 1, 3):
        at = att.at[line, ten]
        copy = remote(at, at, a_send.at[j, 0], a_recv.at[line, ten], line_peer(j), ten)
        copy.start()
        sent.append(copy)
    spread(att, a_send, a_recv, 0)

    slots = seq * SLOT_DEV + lax.broadcasted_iota(jnp.int32, (SLOT_DEV, 1), 0)
    source_of = jnp.full((SLOT_DEV, 1), -1, jnp.int32)
    page = jnp.int32(0)
    for p in range(n_prompts):
        length = len_ref[p]
        within = slots - page
        live = (within >= 0) & (within < length)
        source_of = jnp.where(live, within + starts[p], source_of)
        page = page + (length + PAGE - 1) // PAGE * PAGE
    picked = jnp.zeros((SLOT_DEV, 2 * HD), jnp.float32)

    def pick(c, picked):
        at = pl.ds(pl.multiple_of(c * KEYS, KEYS), KEYS)
        where = c * KEYS + lax.broadcasted_iota(jnp.int32, (SLOT_DEV, KEYS), 1)
        hot = jnp.where(where == source_of, 1.0, 0.0).astype(jnp.bfloat16)
        return picked + jnp.dot(hot, kv[at, :], preferred_element_type=jnp.float32)

    picked = lax.fori_loop(0, tokens // KEYS, pick, picked)
    ck_ref[...] = picked[:, :HD].astype(jnp.bfloat16)
    cv_ref[...] = picked[:, HD:].astype(jnp.bfloat16)

    def w_wait():
        owner = line * rest + ten // parts
        for k in range(n_tensor):

            @pl.when((owner == seq) & (ten == k))
            def _(k=k):
                pltpu.make_async_copy(
                    w_ref.at[:, pl.ds(0, width)], wbuf.at[k], w_local
                ).wait()

            @pl.when((owner != seq) | (ten != k))
            def _(k=k):
                remote(
                    w_ref.at[:, pl.ds(0, width)],
                    wbuf.at[k],
                    w_send.at[0, 0],
                    w_recv.at[k],
                    seq,
                    ten,
                ).wait_recv()

    def multiply(j):
        at_line = (line + j) % LINE
        total = jnp.zeros((rows, width), jnp.float32)

        def add(k, total):
            return total + jnp.dot(
                att[at_line, k], wbuf[k], preferred_element_type=jnp.float32
            )

        total = lax.fori_loop(0, n_tensor, add, total)
        if j == 0:
            proj[line, ten] = total.astype(jnp.bfloat16)
            spread(proj, p_send, p_recv, 0)
        else:
            prod[j] = total.astype(jnp.bfloat16)
            copy = remote(
                prod.at[j],
                proj.at[line, ten],
                p_send.at[j, 0],
                p_recv.at[line, ten],
                line_peer(j),
                ten,
            )
            copy.start()
            sent.append(copy)

    order = (0, 1, 3, 2)
    for n in range(LINE + 1):
        if n + 1 < LINE:
            arrive(att, a_send, a_recv, order[n + 1])
        if n < LINE:
            relay(att, a_send, a_recv, order[n])
        if n == 0:
            w_wait()
        if n < LINE:
            settle(att, a_send, a_recv, order[n])
            multiply(order[n])
    for n in range(1, LINE):
        arrive(proj, p_send, p_recv, order[n])
        relay(proj, p_send, p_recv, order[n - 1])
    relay(proj, p_send, p_recv, order[LINE - 1])
    res_copy.wait()
    for n in range(LINE):
        settle(proj, p_send, p_recv, order[n])

    columns = LINE * n_tensor * width

    def finish(r, carry):
        at = pl.ds(pl.multiple_of(r * ROW_TILE, ROW_TILE), ROW_TILE)
        square = jnp.zeros((ROW_TILE, width), jnp.float32)
        for a in range(LINE):
            for t in range(n_tensor):
                lo = (a * n_tensor + t) * width
                hidden = res[at, lo : lo + width].astype(jnp.float32) + proj[a, t, at, :].astype(
                    jnp.float32
                )
                square = square + hidden * hidden
        factor = lax.rsqrt(jnp.sum(square, axis=1, keepdims=True) * (1.0 / columns) + 1e-05)
        for a in range(LINE):
            for t in range(n_tensor):
                lo = (a * n_tensor + t) * width
                hidden = res[at, lo : lo + width].astype(jnp.float32) + proj[a, t, at, :].astype(
                    jnp.float32
                )
                gain = gain_ref[:, lo : lo + width].astype(jnp.float32)
                normed_ref[at, lo : lo + width] = (hidden * factor * gain).astype(jnp.bfloat16)
        return carry

    lax.fori_loop(0, rows // ROW_TILE, finish, 0)

    for copy in sent:
        copy.wait_send()
    for i in range(rest):
        for k in range(parts):
            target = col * parts + k
            copy = remote(
                w_ref.at[:, pl.ds(k * width, width)],
                wbuf.at[ten],
                w_send.at[i, k],
                w_recv.at[ten],
                col_peer(i),
                target,
            )
            if i == 0:

                @pl.when(target != ten)
                def _(copy=copy):
                    copy.wait_send()

            else:
                copy.wait_send()


def body(
    n_seq, n_tensor, queries, key_rows, value_rows, out_weight, residual_in, norm_gain, lengths
):
    rows, model = residual_in.shape
    width = model // (LINE * n_tensor)
    rest, pairs = n_seq // LINE, n_tensor // CORES
    parts = out_weight.shape[1] // width
    half = rows // 2
    stack = queries.shape[1] // HD * half
    depth = out_weight.shape[0]
    vmem = pl.BlockSpec(memory_space=pltpu.VMEM)
    hbm = pl.BlockSpec(memory_space=pl.ANY)
    dma = pltpu.SemaphoreType.DMA
    return pl.pallas_call(
        functools.partial(kernel, n_seq, n_tensor),
        out_shape=(
            jax.ShapeDtypeStruct((rows, model), jnp.bfloat16),
            jax.ShapeDtypeStruct((SLOT_DEV, HD), jnp.bfloat16),
            jax.ShapeDtypeStruct((SLOT_DEV, HD), jnp.bfloat16),
        ),
        in_specs=[vmem, vmem, vmem, hbm, hbm, vmem, pl.BlockSpec(memory_space=pltpu.SMEM)],
        out_specs=(vmem, vmem, vmem),
        scratch_shapes=[
            pltpu.VMEM((rows * n_seq, 2 * HD), jnp.bfloat16),
            pltpu.VMEM((n_tensor, depth, width), jnp.bfloat16),
            pltpu.VMEM((LINE, n_tensor, rows, depth), jnp.bfloat16),
            pltpu.VMEM((LINE, rows, width), jnp.bfloat16),
            pltpu.VMEM((LINE, n_tensor, rows, width), jnp.bfloat16),
            pltpu.VMEM((rows, model), jnp.bfloat16),
            pltpu.VMEM((stack, HD), jnp.float32),
            pltpu.VMEM((stack, HD), jnp.float32),
            pltpu.VMEM((stack, HD), jnp.float32),
            dma((LINE, rest, 2)),
            dma((n_seq, 2)),
            dma((rest, parts)),
            dma((n_tensor,)),
            dma,
            dma((LINE, 2 * pairs)),
            dma((LINE, n_tensor)),
            dma((LINE, 2 * pairs)),
            dma((LINE, n_tensor)),
            dma,
        ],
        compiler_params=pltpu.CompilerParams(
            collective_id=0, has_side_effects=True, vmem_limit_bytes=58 * 2**20
        ),
        cost_estimate=pl.CostEstimate(
            flops=5 * 10**9, bytes_accessed=14 * 10**6, transcendentals=2 * 10**6
        ),
    )(
        queries,
        key_rows,
        value_rows,
        out_weight,
        residual_in,
        norm_gain.reshape(1, model),
        lengths,
    )


def solution(mesh):
    return jax.shard_map(
        functools.partial(body, mesh.shape["seq"], mesh.shape["tensor"]),
        mesh=mesh,
        in_specs=(
            P("seq", "tensor"),
            P("seq", "tensor"),
            P("seq", "tensor"),
            P("tensor", "seq"),
            P("seq", None),
            P(),
            P(),
        ),
        out_specs=(P("seq", None), P("seq", "tensor"), P("seq", "tensor")),
        check_vma=False,
    )
```

time: 277 us -> 169 us (0.61)
  the two profiles are of different devices: /device:TPU:0 before, /device:TPU:5 now
where the time goes in v1:
time: 169 us
  Pallas kernels  160 us (95%)
  local copies, waits for them, and re-layouts  8.18 us (5%)
    pallas_call x1, Pallas kernels, body(): pl.pallas_call(functools.partial(kernel, n_seq, n_tensor), out_shape=(jax...  160 us
    unnamed x7, local copies, waits for them, and re-layouts  6.83 us

profile of v1, /device:TPU:5, one launch (start us, length us, event | category | flops | bytes accessed | tf_op | source)
XLA Modules:
  0.0 168.9 jit_solution(12288082930801992250)
XLA Ops:
  0.6 1.4 reshape.9.gain_ref
  2.0 160.0 %shard_map.94 = (bf16[320,8192]{1,0:T(8,128)(2,1)}, bf16[704,128]{1,0:T(8,128)(2,1)}, bf16[704,128]{1,0:T(8,128)(2,1)}) custom-call(bf16[320,512]{1,0:T(8,128)(2,1)} %q_ref.1, bf16[320,128]{1,0:T(8,128)(2,1)} %k_ref.1, bf16[320,128]{1,0:T(8,128)(2,1)} %v_ref.1, bf16[512,1024]{1,0:T(8,128)(2,1)} %w_ref.1, bf16[320,8192]{1,0:T(8,128)(2,1)} %res_ref.1, ...), custom_call_target="tpu_custom_call" | custom-call | flops 5000000000 | bytes 14000000 | tf_op jit(solution)/shard_map/pallas_call | solution.py:410
  162.0 0.0 copy-start.1
  162.0 0.0 copy-start
  162.0 5.5 %copy.13 = bf16[320,8192]{1,0:T(8,128)(2,1)} copy(bf16[320,8192]{1,0:T(8,128)(2,1)} %get-tuple-element.6) | data formatting | bytes 10485760
  167.5 0.0 copy-done.1
  167.5 0.7 copy.14
  168.2 0.0 copy-done
  168.2 0.7 copy.15
Async XLA Ops:
  162.0 5.5 %copy-start.1 = (bf16[704,128]{1,0:T(8,128)(2,1)S(1)}, bf16[704,128]{1,0:T(8,128)(2,1)}, u32[]{:S(2)}) copy-start(bf16[704,128]{1,0:T(8,128)(2,1)} %get-tuple-element.7) | copy-start | bytes 540676
  162.0 6.2 %copy-start = (bf16[704,128]{1,0:T(8,128)(2,1)S(1)}, bf16[704,128]{1,0:T(8,128)(2,1)}, u32[]{:S(2)}) copy-start(bf16[704,128]{1,0:T(8,128)(2,1)} %get-tuple-element.8) | copy-start | bytes 540676

commit v2 on v1

v2 whole, which is shorter than its diff:
```python
import functools
import math

import jax
import jax.numpy as jnp
from jax import lax
from jax.experimental import pallas as pl
from jax.experimental.pallas import tpu as pltpu
from jax.sharding import PartitionSpec as P

HD = 128
PAGE = 128
SLOT_DEV = 704
LINE = 4
CORES = 2
KEYS = 256
ROW_TILE = 16
MESH = pl.DeviceIdType.MESH


def kernel(
    n_seq,
    n_tensor,
    q_ref,
    k_ref,
    v_ref,
    w_ref,
    res_ref,
    gain_ref,
    len_ref,
    normed_ref,
    ck_ref,
    cv_ref,
    kv,
    wbuf,
    att,
    prod,
    proj,
    res,
    m_ref,
    l_ref,
    acc_ref,
    kv_send,
    kv_recv,
    w_send,
    w_recv,
    w_local,
    w_across,
    w_crossed,
    a_send,
    a_recv,
    p_send,
    p_recv,
    res_sem,
):
    rest = n_seq // LINE
    pairs = n_tensor // CORES
    rows = q_ref.shape[0]
    half = rows // 2
    tokens = kv.shape[0]
    heads = q_ref.shape[1] // HD
    width = wbuf.shape[3]
    parts = w_ref.shape[1] // width
    n_prompts = len_ref.shape[0]

    seq = lax.axis_index("seq")
    ten = lax.axis_index("tensor")
    line = seq % LINE
    col = seq // LINE
    pair = ten // CORES
    core = ten % CORES

    def line_peer(j):
        return col * LINE + (line + j) % LINE

    def col_peer(i):
        return ((col + i) % rest) * LINE + line

    def pair_peer(i):
        return ((pair + i) % pairs) * CORES + core

    twin = pair * CORES + 1 - core

    def remote(src, dst, send, recv, to_seq, to_ten):
        return pltpu.make_async_remote_copy(
            src_ref=src,
            dst_ref=dst,
            send_sem=send,
            recv_sem=recv,
            device_id=(to_seq, to_ten),
            device_id_type=MESH,
        )

    res_copy = pltpu.make_async_copy(res_ref, res, res_sem)
    res_copy.start()

    barrier = pltpu.get_barrier_semaphore()
    peers = [(line_peer(j), ten) for j in range(1, LINE)]
    peers += [(col_peer(i), ten) for i in range(1, rest)]
    peers += [(seq, (ten + k) % n_tensor) for k in range(1, n_tensor)]
    for peer in peers:
        pl.semaphore_signal(barrier, inc=1, device_id=peer, device_id_type=MESH)

    def kv_rows(source, h):
        block = source if h == 0 else 2 * n_seq - 1 - source
        return pl.ds(pl.multiple_of(block * half, half), half)

    for h in range(2):
        kv[kv_rows(seq, h), :HD] = k_ref[h * half : (h + 1) * half, :]
        kv[kv_rows(seq, h), HD:] = v_ref[h * half : (h + 1) * half, :]
    pl.semaphore_wait(barrier, len(peers))

    sent = []

    def kv_copy(source, h, i, j, to_seq):
        at = kv.at[kv_rows(source, h)]
        return remote(at, at, kv_send.at[i, j, h], kv_recv.at[source, h], to_seq, ten)

    def kv_start(source, h, i, j, to_seq):
        copy = kv_copy(source, h, i, j, to_seq)
        copy.start()
        sent.append(copy)

    for h in range(2):
        for i in range(1, rest):
            kv_start(seq, h, i, 0, col_peer(i))
        for j in (2, 1, 3):
            kv_start(seq, h, 0, j, line_peer(j))

    base = col // 2 * parts
    slot = col % 2
    holds = (base <= ten) & (ten < base + parts)
    always = parts == n_tensor

    def guarded(condition, action):
        if always:
            action()
        else:
            pl.when(condition)(action)

    def w_part(k):
        index = (ten + k) % parts
        piece = w_ref.at[:, pl.ds(pl.multiple_of(index * width, width), width)]
        return piece, base + index

    def w_first(k):
        piece, target = w_part(k)
        return remote(piece, wbuf.at[slot, ten], w_send.at[k], w_recv.at[ten], seq, target)

    def w_keep():
        return pltpu.make_async_copy(w_part(0)[0], wbuf.at[slot, ten], w_local)

    guarded(holds, lambda: w_keep().start())
    if not always:
        pl.when(jnp.logical_not(holds))(lambda: w_first(0).start())
    for k in range(1, parts):
        w_first(k).start()

    for i in range(1, rest):
        source = col_peer(i)
        for h in range(2):
            kv_copy(source, h, i, 0, seq).wait_recv()
            for j in (2, 1, 3):
                kv_start(source, h, i, j, line_peer(j))

    def w_second(i):
        return remote(
            wbuf.at[slot], wbuf.at[slot], w_across.at[i], w_crossed.at[slot], col_peer(i), ten
        )

    def w_relay():
        w_keep().wait()
        for k in range(1, n_tensor):
            source = (ten + k) % n_tensor
            remote(
                w_part(0)[0], wbuf.at[slot, source], w_send.at[0], w_recv.at[source], seq, ten
            ).wait_recv()
        for i in range(1, rest):
            w_second(i).start()

    guarded(holds, w_relay)

    def w_wait(u):
        owner = ten // parts * 2 + u

        @pl.when(owner != col)
        def _():
            remote(
                wbuf.at[u], wbuf.at[u], w_across.at[0], w_crossed.at[u], seq, ten
            ).wait_recv()

    starts = [jnp.int32(0)]
    for p in range(n_prompts - 1):
        starts.append(starts[-1] + len_ref[p])

    def kv_wait(h):
        for i in range(rest):
            for j in range(1, LINE):
                source = ((col + i) % rest) * LINE + (line + j) % LINE
                kv_copy(source, h, i, j, seq).wait_recv()

    def att_at(h, at_line, at_ten):
        return att.at[at_line, at_ten, pl.ds(h * half, half)]

    def proj_at(u, at_line, at_ten):
        return proj.at[u, at_line, at_ten]

    def piece_copy(where, n, send, recv, at_line, at_ten, slot, to_ten):
        at = where(n, at_line, at_ten)
        return remote(at, at, send.at[(n,) + slot], recv.at[n, at_line, at_ten], seq, to_ten)

    def spread(where, n, send, recv, j):
        at_line = (line + j) % LINE
        for i in range(1, pairs):
            copy = piece_copy(where, n, send, recv, at_line, ten, (j, i), pair_peer(i))
            copy.start()
            sent.append(copy)
        copy = piece_copy(where, n, send, recv, at_line, ten, (j, pairs), twin)
        copy.start()
        sent.append(copy)

    def relay(where, n, send, recv, j):
        at_line = (line + j) % LINE
        for i in range(1, pairs):
            source = pair_peer(pairs - i)
            piece_copy(where, n, send, recv, at_line, source, (j, 0), ten).wait_recv()
            copy = piece_copy(where, n, send, recv, at_line, source, (j, pairs + i), twin)
            copy.start()
            sent.append(copy)

    def settle(where, n, send, recv, j):
        at_line = (line + j) % LINE
        for y in range(pairs):
            source = y * CORES + 1 - core
            piece_copy(where, n, send, recv, at_line, source, (j, 0), ten).wait_recv()

    def arrive(where, n, send, recv, j):
        at_line = (line + j) % LINE
        piece_copy(where, n, send, recv, at_line, ten, (j, 0), ten).wait_recv()
        spread(where, n, send, recv, j)

    scale = 1.0 / math.sqrt(HD)
    for h in range(2):
        kv_wait(h)
        block = seq if h == 0 else 2 * n_seq - 1 - seq
        query = jnp.concatenate(
            [q_ref[h * half : (h + 1) * half, g * HD : (g + 1) * HD] for g in range(heads)], axis=0
        )
        position = block * half + lax.broadcasted_iota(jnp.int32, (half, 1), 0)
        begin = jnp.zeros((half, 1), jnp.int32)
        for p in range(1, n_prompts):
            begin = jnp.where(starts[p] <= position, starts[p], begin)
        m_ref[...] = jnp.full_like(m_ref, -1e20)
        l_ref[...] = jnp.zeros_like(l_ref)
        acc_ref[...] = jnp.zeros_like(acc_ref)

        def step(c, carry, query=query, position=position, begin=begin):
            at = pl.ds(pl.multiple_of(c * KEYS, KEYS), KEYS)
            scores = lax.dot_general(
                query,
                kv[at, :HD],
                (((1,), (1,)), ((), ())),
                preferred_element_type=jnp.float32,
            )
            where = c * KEYS + lax.broadcasted_iota(jnp.int32, (half, KEYS), 1)
            bias = jnp.where((where >= begin) & (where <= position), 0.0, -1e30)
            scores = scores * scale + jnp.concatenate([bias] * heads, axis=0)
            old = m_ref[:, :1]
            top = jnp.maximum(old, jnp.max(scores, axis=1, keepdims=True))
            shrink = jnp.exp(old - top)
            weights = jnp.exp(scores - top)
            total = l_ref[:, :1] * shrink + jnp.sum(weights, axis=1, keepdims=True)
            acc_ref[...] = acc_ref[...] * shrink + jnp.dot(
                weights.astype(jnp.bfloat16), kv[at, HD:], preferred_element_type=jnp.float32
            )
            m_ref[...] = jnp.broadcast_to(top, m_ref.shape)
            l_ref[...] = jnp.broadcast_to(total, l_ref.shape)
            return carry

        lax.fori_loop(0, ((block + 1) * half + KEYS - 1) // KEYS, step, 0)
        result = (acc_ref[...] / l_ref[...]).astype(jnp.bfloat16)
        for g in range(heads):
            att[line, ten, h * half : (h + 1) * half, g * HD : (g + 1) * HD] = result[
                g * half : (g + 1) * half
            ]
        spread(att_at, h, a_send, a_recv, 0)
        for j in (2, 1, 3):
            at = att_at(h, line, ten)
            copy = remote(
                at, at, a_send.at[h, j, 0], a_recv.at[h, line, ten], line_peer(j), ten
            )
            copy.start()
            sent.append(copy)

    slots = seq * SLOT_DEV + lax.broadcasted_iota(jnp.int32, (SLOT_DEV, 1), 0)
    source_of = jnp.full((SLOT_DEV, 1), -1, jnp.int32)
    page = jnp.int32(0)
    for p in range(n_prompts):
        length = len_ref[p]
        within = slots - page
        live = (within >= 0) & (within < length)
        source_of = jnp.where(live, within + starts[p], source_of)
        page = page + (length + PAGE - 1) // PAGE * PAGE
    picked = jnp.zeros((SLOT_DEV, 2 * HD), jnp.float32)

    def pick(c, picked):
        at = pl.ds(pl.multiple_of(c * KEYS, KEYS), KEYS)
        where = c * KEYS + lax.broadcasted_iota(jnp.int32, (SLOT_DEV, KEYS), 1)
        hot = jnp.where(where == source_of, 1.0, 0.0).astype(jnp.bfloat16)
        return picked + jnp.dot(hot, kv[at, :], preferred_element_type=jnp.float32)

    picked = lax.fori_loop(0, tokens // KEYS, pick, picked)
    ck_ref[...] = picked[:, :HD].astype(jnp.bfloat16)
    cv_ref[...] = picked[:, HD:].astype(jnp.bfloat16)

    def multiply(u, j):
        at_line = (line + j) % LINE

        def add(k, total):
            return total + jnp.dot(
                att[at_line, k], wbuf[u, k], preferred_element_type=jnp.float32
            )

        total = lax.fori_loop(0, n_tensor, add, jnp.zeros((rows, width), jnp.float32))
        if j == 0:
            proj[u, line, ten] = total.astype(jnp.bfloat16)
            spread(proj_at, u, p_send, p_recv, 0)
        else:
            prod[u, j] = total.astype(jnp.bfloat16)
            copy = remote(
                prod.at[u, j],
                proj.at[u, line, ten],
                p_send.at[u, j, 0],
                p_recv.at[u, line, ten],
                line_peer(j),
                ten,
            )
            copy.start()
            sent.append(copy)

    order = (0, 2, 1, 3)
    other = 1 - slot
    w_wait(slot)
    for n in range(LINE):
        for h in range(2):
            if n + 1 < LINE:
                arrive(att_at, h, a_send, a_recv, order[n + 1])
            relay(att_at, h, a_send, a_recv, order[n])
        for h in range(2):
            settle(att_at, h, a_send, a_recv, order[n])
        multiply(slot, order[n])
    w_wait(other)
    for u, last in ((slot, False), (other, True)):
        for n in range(LINE):
            if not last:
                multiply(other, order[n])
            if n + 1 < LINE:
                arrive(proj_at, u, p_send, p_recv, order[n + 1])
            relay(proj_at, u, p_send, p_recv, order[n])
    res_copy.wait()
    for u in (slot, other):
        for n in range(LINE):
            settle(proj_at, u, p_send, p_recv, order[n])

    columns = res.shape[1]
    places = [
        (u, a, t, (((t // parts * 2 + u) * LINE + a) * parts + t % parts) * width)
        for u in range(2)
        for a in range(LINE)
        for t in range(n_tensor)
    ]

    def finish(r, carry):
        at = pl.ds(pl.multiple_of(r * ROW_TILE, ROW_TILE), ROW_TILE)
        square = jnp.zeros((ROW_TILE, width), jnp.float32)
        for u, a, t, lo in places:
            hidden = res[at, lo : lo + width].astype(jnp.float32) + proj[u, a, t, at, :].astype(
                jnp.float32
            )
            square = square + hidden * hidden
        factor = lax.rsqrt(jnp.sum(square, axis=1, keepdims=True) * (1.0 / columns) + 1e-05)
        for u, a, t, lo in places:
            hidden = res[at, lo : lo + width].astype(jnp.float32) + proj[u, a, t, at, :].astype(
                jnp.float32
            )
            gain = gain_ref[:, lo : lo + width].astype(jnp.float32)
            normed_ref[at, lo : lo + width] = (hidden * factor * gain).astype(jnp.bfloat16)
        return carry

    lax.fori_loop(0, rows // ROW_TILE, finish, 0)

    for copy in sent:
        copy.wait_send()
    for k in range(1, parts):
        w_first(k).wait_send()
    if not always:
        pl.when(jnp.logical_not(holds))(lambda: w_first(0).wait_send())

    def w_sent():
        for i in range(1, rest):
            w_second(i).wait_send()

    guarded(holds, w_sent)


def body(
    n_seq, n_tensor, queries, key_rows, value_rows, out_weight, residual_in, norm_gain, lengths
):
    rows, model = residual_in.shape
    width = model // (LINE * n_tensor) // 2
    rest, pairs = n_seq // LINE, n_tensor // CORES
    parts = out_weight.shape[1] // width
    half = rows // 2
    stack = queries.shape[1] // HD * half
    depth = out_weight.shape[0]
    vmem = pl.BlockSpec(memory_space=pltpu.VMEM)
    hbm = pl.BlockSpec(memory_space=pl.ANY)
    dma = pltpu.SemaphoreType.DMA
    return pl.pallas_call(
        functools.partial(kernel, n_seq, n_tensor),
        out_shape=(
            jax.ShapeDtypeStruct((rows, model), jnp.bfloat16),
            jax.ShapeDtypeStruct((SLOT_DEV, HD), jnp.bfloat16),
            jax.ShapeDtypeStruct((SLOT_DEV, HD), jnp.bfloat16),
        ),
        in_specs=[vmem, vmem, vmem, hbm, hbm, vmem, pl.BlockSpec(memory_space=pltpu.SMEM)],
        out_specs=(vmem, vmem, vmem),
        scratch_shapes=[
            pltpu.VMEM((rows * n_seq, 2 * HD), jnp.bfloat16),
            pltpu.VMEM((2, n_tensor, depth, width), jnp.bfloat16),
            pltpu.VMEM((LINE, n_tensor, rows, depth), jnp.bfloat16),
            pltpu.VMEM((2, LINE, rows, width), jnp.bfloat16),
            pltpu.VMEM((2, LINE, n_tensor, rows, width), jnp.bfloat16),
            pltpu.VMEM((rows, model), jnp.bfloat16),
            pltpu.VMEM((stack, HD), jnp.float32),
            pltpu.VMEM((stack, HD), jnp.float32),
            pltpu.VMEM((stack, HD), jnp.float32),
            dma((rest, LINE, 2)),
            dma((n_seq, 2)),
            dma((parts,)),
            dma((n_tensor,)),
            dma,
            dma((rest,)),
            dma((2,)),
            dma((2, LINE, 2 * pairs)),
            dma((2, LINE, n_tensor)),
            dma((2, LINE, 2 * pairs)),
            dma((2, LINE, n_tensor)),
            dma,
        ],
        compiler_params=pltpu.CompilerParams(
            collective_id=0, has_side_effects=True, vmem_limit_bytes=58 * 2**20
        ),
        cost_estimate=pl.CostEstimate(
            flops=5 * 10**9, bytes_accessed=14 * 10**6, transcendentals=2 * 10**6
        ),
    )(
        queries,
        key_rows,
        value_rows,
        out_weight,
        residual_in,
        norm_gain.reshape(1, model),
        lengths,
    )


def solution(mesh):
    return jax.shard_map(
        functools.partial(body, mesh.shape["seq"], mesh.shape["tensor"]),
        mesh=mesh,
        in_specs=(
            P("seq", "tensor"),
            P("seq", "tensor"),
            P("seq", "tensor"),
            P("tensor", "seq"),
            P("seq", None),
            P(),
            P(),
        ),
        out_specs=(P("seq", None), P("seq", "tensor"), P("seq", "tensor")),
        check_vma=False,
    )
```

time: 169 us -> 139 us (0.82)
  the two profiles are of different devices: /device:TPU:5 before, /device:TPU:0 now
where the time goes in v2:
time: 139 us; the launch traced here: 137 us
  Pallas kernels  129 us (93%)
  local copies, waits for them, and re-layouts  8.18 us (6%)
    pallas_call x1, Pallas kernels, body(): pl.pallas_call(functools.partial(kernel, n_seq, n_tensor), out_shape=(jax...  129 us
    unnamed x7, local copies, waits for them, and re-layouts  6.83 us

profile of v2, /device:TPU:0, one launch (start us, length us, event | category | flops | bytes accessed | tf_op | source)
XLA Modules:
  0.0 137.4 jit_solution(18224872102969341173)
XLA Ops:
  0.6 1.4 reshape.9.gain_ref
  2.0 128.6 %shard_map.94 = (bf16[320,8192]{1,0:T(8,128)(2,1)}, bf16[704,128]{1,0:T(8,128)(2,1)}, bf16[704,128]{1,0:T(8,128)(2,1)}) custom-call(bf16[320,512]{1,0:T(8,128)(2,1)} %q_ref.1, bf16[320,128]{1,0:T(8,128)(2,1)} %k_ref.1, bf16[320,128]{1,0:T(8,128)(2,1)} %v_ref.1, bf16[512,1024]{1,0:T(8,128)(2,1)} %w_ref.1, bf16[320,8192]{1,0:T(8,128)(2,1)} %res_ref.1, ...), custom_call_target="tpu_custom_call" | custom-call | flops 5000000000 | bytes 14000000 | tf_op jit(solution)/shard_map/pallas_call | solution.py:419
  130.6 0.0 copy-start.1
  130.6 0.0 copy-start
  130.6 5.5 %copy.13 = bf16[320,8192]{1,0:T(8,128)(2,1)} copy(bf16[320,8192]{1,0:T(8,128)(2,1)} %get-tuple-element.6) | data formatting | bytes 10485760
  136.1 0.0 copy-done.1
  136.1 0.7 copy.14
  136.8 0.0 copy-done
  136.8 0.7 copy.15
Async XLA Ops:
  130.6 5.5 %copy-start.1 = (bf16[704,128]{1,0:T(8,128)(2,1)S(1)}, bf16[704,128]{1,0:T(8,128)(2,1)}, u32[]{:S(2)}) copy-start(bf16[704,128]{1,0:T(8,128)(2,1)} %get-tuple-element.7) | copy-start | bytes 540676
  130.6 6.2 %copy-start = (bf16[704,128]{1,0:T(8,128)(2,1)S(1)}, bf16[704,128]{1,0:T(8,128)(2,1)}, u32[]{:S(2)}) copy-start(bf16[704,128]{1,0:T(8,128)(2,1)} %get-tuple-element.8) | copy-start | bytes 540676

commit v3 on v2

--- a/solution.py
+++ b/solution.py
@@ -150,11 +150,28 @@
     def w_keep():
         return pltpu.make_async_copy(w_part(0)[0], wbuf.at[slot, ten], w_local)
 
-    guarded(holds, lambda: w_keep().start())
+    def w_second(i, k):
+        source = (ten + k) % n_tensor
+        at = wbuf.at[slot, source]
+        return remote(
+            w_part(0)[0] if k == 0 else at,
+            at,
+            w_across.at[i, k],
+            w_crossed.at[slot, source],
+            col_peer(i),
+            ten,
+        )
+
+    def w_begin():
+        w_keep().start()
+        for i in range(1, rest):
+            w_second(i, 0).start()
+
     if not always:
         pl.when(jnp.logical_not(holds))(lambda: w_first(0).start())
     for k in range(1, parts):
         w_first(k).start()
+    guarded(holds, w_begin)
 
     for i in range(1, rest):
         source = col_peer(i)
@@ -163,20 +180,15 @@
             for j in (2, 1, 3):
                 kv_start(source, h, i, j, line_peer(j))
 
-    def w_second(i):
-        return remote(
-            wbuf.at[slot], wbuf.at[slot], w_across.at[i], w_crossed.at[slot], col_peer(i), ten
-        )
-
     def w_relay():
-        w_keep().wait()
         for k in range(1, n_tensor):
             source = (ten + k) % n_tensor
             remote(
                 w_part(0)[0], wbuf.at[slot, source], w_send.at[0], w_recv.at[source], seq, ten
             ).wait_recv()
-        for i in range(1, rest):
-            w_second(i).start()
+            for i in range(1, rest):
+                w_second(i, k).start()
+        w_keep().wait()
 
     guarded(holds, w_relay)
 
@@ -185,9 +197,9 @@
 
         @pl.when(owner != col)
         def _():
-            remote(
-                wbuf.at[u], wbuf.at[u], w_across.at[0], w_crossed.at[u], seq, ten
-            ).wait_recv()
+            for k in range(n_tensor):
+                at = wbuf.at[u, k]
+                remote(at, at, w_across.at[0, 0], w_crossed.at[u, k], seq, ten).wait_recv()
 
     starts = [jnp.int32(0)]
     for p in range(n_prompts - 1):
@@ -238,6 +250,26 @@
         at_line = (line + j) % LINE
         piece_copy(where, n, send, recv, at_line, ten, (j, 0), ten).wait_recv()
         spread(where, n, send, recv, j)
+
+    def att_copy(h, j, y, slot, to_seq, to_ten):
+        at_line, at_ten = (line + j) % LINE, pair_peer(y)
+        at = att_at(h, at_line, at_ten)
+        return remote(
+            at, at, a_send.at[(h,) + slot], a_recv.at[h, at_line, at_ten], to_seq, to_ten
+        )
+
+    def att_send(h, j, y, slot, to_seq, to_ten):
+        copy = att_copy(h, j, y, slot, to_seq, to_ten)
+        copy.start()
+        sent.append(copy)
+
+    def att_round(h, y):
+        for j in (2, 1, 3):
+            att_send(h, 0, y, (j, y), line_peer(j), ten)
+        att_send(h, 0, y, (0, pairs + y), seq, twin)
+
+    def att_arrive(h, j, y):
+        att_copy(h, j, y, (0, 0), seq, ten).wait_recv()
 
     scale = 1.0 / math.sqrt(HD)
     for h in range(2):
@@ -283,14 +315,9 @@
             att[line, ten, h * half : (h + 1) * half, g * HD : (g + 1) * HD] = result[
                 g * half : (g + 1) * half
             ]
-        spread(att_at, h, a_send, a_recv, 0)
-        for j in (2, 1, 3):
-            at = att_at(h, line, ten)
-            copy = remote(
-                at, at, a_send.at[h, j, 0], a_recv.at[h, line, ten], line_peer(j), ten
-            )
-            copy.start()
-            sent.append(copy)
+        for i in range(1, pairs):
+            att_send(h, 0, 0, (0, i), seq, pair_peer(i))
+        att_round(h, 0)
 
     slots = seq * SLOT_DEV + lax.broadcasted_iota(jnp.int32, (SLOT_DEV, 1), 0)
     source_of = jnp.full((SLOT_DEV, 1), -1, jnp.int32)
@@ -341,11 +368,16 @@
     order = (0, 2, 1, 3)
     other = 1 - slot
     w_wait(slot)
+    for h in range(2):
+        for y in range(1, pairs):
+            att_arrive(h, 0, y)
+            att_round(h, y)
     for n in range(LINE):
         for h in range(2):
-            if n + 1 < LINE:
-                arrive(att_at, h, a_send, a_recv, order[n + 1])
-            relay(att_at, h, a_send, a_recv, order[n])
+            for y in range(pairs):
+                if n > 0:
+                    att_arrive(h, order[n], y)
+                    att_send(h, order[n], y, (order[n], pairs + y), seq, twin)
         for h in range(2):
             settle(att_at, h, a_send, a_recv, order[n])
         multiply(slot, order[n])
@@ -398,7 +430,8 @@
 
     def w_sent():
         for i in range(1, rest):
-            w_second(i).wait_send()
+            for k in range(n_tensor):
+                w_second(i, k).wait_send()
 
     guarded(holds, w_sent)
 
@@ -440,8 +473,8 @@
             dma((parts,)),
             dma((n_tensor,)),
             dma,
-            dma((rest,)),
-            dma((2,)),
+            dma((rest, n_tensor)),
+            dma((2, n_tensor)),
             dma((2, LINE, 2 * pairs)),
             dma((2, LINE, n_tensor)),
             dma((2, LINE, 2 * pairs)),

time: 139 us -> 134 us (0.964)
  Pallas kernels: 129 us -> 124 us
    pallas_call x1, Pallas kernels: 129 us -> 124 us  [body(): pl.pallas_call(functools.partial(kernel, n_seq, n_tensor), out_shape=(jax...]
where the time goes in v3:
time: 134 us; the launch traced here: 133 us
  Pallas kernels  124 us (93%)
  local copies, waits for them, and re-layouts  8.18 us (6%)
    pallas_call x1, Pallas kernels, body(): pl.pallas_call(functools.partial(kernel, n_seq, n_tensor), out_shape=(jax...  124 us
    unnamed x7, local copies, waits for them, and re-layouts  6.83 us

profile of v3, /device:TPU:0, one launch (start us, length us, event | category | flops | bytes accessed | tf_op | source)
XLA Modules:
  0.0 132.6 jit_solution(310388142929995762)
XLA Ops:
  0.6 1.4 %reshape.9.gain_ref = bf16[1,8192]{1,0:T(2,128)(2,1)} reshape(bf16[8192]{0:T(1024)(128)(2,1)} %param.12) | data formatting | bytes 32768 | tf_op jit(solution)/shard_map/reshape | solution.py:496
  2.0 123.8 %shard_map.94 = (bf16[320,8192]{1,0:T(8,128)(2,1)}, bf16[704,128]{1,0:T(8,128)(2,1)}, bf16[704,128]{1,0:T(8,128)(2,1)}) custom-call(bf16[320,512]{1,0:T(8,128)(2,1)} %q_ref.1, bf16[320,128]{1,0:T(8,128)(2,1)} %k_ref.1, bf16[320,128]{1,0:T(8,128)(2,1)} %v_ref.1, bf16[512,1024]{1,0:T(8,128)(2,1)} %w_ref.1, bf16[320,8192]{1,0:T(8,128)(2,1)} %res_ref.1, ...), custom_call_target="tpu_custom_call" | custom-call | flops 5000000000 | bytes 14000000 | tf_op jit(solution)/shard_map/pallas_call | solution.py:452
  125.8 0.0 copy-start.1
  125.8 0.0 copy-start
  125.8 5.5 %copy.13 = bf16[320,8192]{1,0:T(8,128)(2,1)} copy(bf16[320,8192]{1,0:T(8,128)(2,1)} %get-tuple-element.6) | data formatting | bytes 10485760
  131.3 0.0 copy-done.1
  131.3 0.7 copy.14
  132.0 0.0 copy-done
  132.0 0.7 copy.15
Async XLA Ops:
  125.8 5.5 %copy-start.1 = (bf16[704,128]{1,0:T(8,128)(2,1)S(1)}, bf16[704,128]{1,0:T(8,128)(2,1)}, u32[]{:S(2)}) copy-start(bf16[704,128]{1,0:T(8,128)(2,1)} %get-tuple-element.7) | copy-start | bytes 540676
  125.8 6.2 %copy-start = (bf16[704,128]{1,0:T(8,128)(2,1)S(1)}, bf16[704,128]{1,0:T(8,128)(2,1)}, u32[]{:S(2)}) copy-start(bf16[704,128]{1,0:T(8,128)(2,1)} %get-tuple-element.8) | copy-start | bytes 540676

commit v4 on v3

--- a/solution.py
+++ b/solution.py
@@ -14,7 +14,6 @@
 LINE = 4
 CORES = 2
 KEYS = 256
-ROW_TILE = 16
 MESH = pl.DeviceIdType.MESH
 
 
@@ -26,9 +25,9 @@
     v_ref,
     w_ref,
     res_ref,
-    gain_ref,
     len_ref,
-    normed_ref,
+    out_ref,
+    factor_ref,
     ck_ref,
     cv_ref,
     kv,
@@ -40,6 +39,7 @@
     m_ref,
     l_ref,
     acc_ref,
+    square,
     kv_send,
     kv_recv,
     w_send,
@@ -52,6 +52,7 @@
     p_send,
     p_recv,
     res_sem,
+    out_sem,
 ):
     rest = n_seq // LINE
     pairs = n_tensor // CORES
@@ -70,8 +71,11 @@
     pair = ten // CORES
     core = ten % CORES
 
+    def place(j):
+        return (line // 2 + j // 2) % 2 * 2 + (line % 2 + j % 2) % 2
+
     def line_peer(j):
-        return col * LINE + (line + j) % LINE
+        return col * LINE + place(j)
 
     def col_peer(i):
         return ((col + i) % rest) * LINE + line
@@ -121,11 +125,17 @@
         copy.start()
         sent.append(copy)
 
+    def kv_source(i, j):
+        return (col + i) % rest * LINE + place(j)
+
+    def kv_square(i, h):
+        kv_start(kv_source(i, 0), h, i, 2, line_peer(2))
+        kv_start(kv_source(i, 0), h, i, 1, line_peer(1))
+
     for h in range(2):
         for i in range(1, rest):
             kv_start(seq, h, i, 0, col_peer(i))
-        for j in (2, 1, 3):
-            kv_start(seq, h, 0, j, line_peer(j))
+        kv_square(0, h)
 
     base = col // 2 * parts
     slot = col % 2
@@ -163,7 +173,6 @@
         )
 
     def w_begin():
-        w_keep().start()
         for i in range(1, rest):
             w_second(i, 0).start()
 
@@ -171,16 +180,26 @@
         pl.when(jnp.logical_not(holds))(lambda: w_first(0).start())
     for k in range(1, parts):
         w_first(k).start()
-    guarded(holds, w_begin)
-
-    for i in range(1, rest):
-        source = col_peer(i)
-        for h in range(2):
-            kv_copy(source, h, i, 0, seq).wait_recv()
-            for j in (2, 1, 3):
-                kv_start(source, h, i, j, line_peer(j))
+    guarded(holds, lambda: w_keep().start())
+
+    def kv_arrive(i, j, h):
+        kv_copy(kv_source(i, j), h, i, j, seq).wait_recv()
+
+    def kv_relay(i, h):
+        kv_arrive(i, 2, h)
+        kv_start(kv_source(i, 2), h, i, 3, line_peer(1))
+
+    for h in range(2):
+        kv_relay(0, h)
+        for i in range(1, rest):
+            kv_arrive(i, 0, h)
+            kv_square(i, h)
+    for h in range(2):
+        for i in range(1, rest):
+            kv_relay(i, h)
 
     def w_relay():
+        w_begin()
         for k in range(1, n_tensor):
             source = (ten + k) % n_tensor
             remote(
@@ -190,8 +209,6 @@
                 w_second(i, k).start()
         w_keep().wait()
 
-    guarded(holds, w_relay)
-
     def w_wait(u):
         owner = ten // parts * 2 + u
 
@@ -207,9 +224,8 @@
 
     def kv_wait(h):
         for i in range(rest):
-            for j in range(1, LINE):
-                source = ((col + i) % rest) * LINE + (line + j) % LINE
-                kv_copy(source, h, i, j, seq).wait_recv()
+            for j in (1, 3):
+                kv_arrive(i, j, h)
 
     def att_at(h, at_line, at_ten):
         return att.at[at_line, at_ten, pl.ds(h * half, half)]
@@ -222,7 +238,7 @@
         return remote(at, at, send.at[(n,) + slot], recv.at[n, at_line, at_ten], seq, to_ten)
 
     def spread(where, n, send, recv, j):
-        at_line = (line + j) % LINE
+        at_line = place(j)
         for i in range(1, pairs):
             copy = piece_copy(where, n, send, recv, at_line, ten, (j, i), pair_peer(i))
             copy.start()
@@ -232,7 +248,7 @@
         sent.append(copy)
 
     def relay(where, n, send, recv, j):
-        at_line = (line + j) % LINE
+        at_line = place(j)
         for i in range(1, pairs):
             source = pair_peer(pairs - i)
             piece_copy(where, n, send, recv, at_line, source, (j, 0), ten).wait_recv()
@@ -241,18 +257,18 @@
             sent.append(copy)
 
     def settle(where, n, send, recv, j):
-        at_line = (line + j) % LINE
+        at_line = place(j)
         for y in range(pairs):
             source = y * CORES + 1 - core
             piece_copy(where, n, send, recv, at_line, source, (j, 0), ten).wait_recv()
 
     def arrive(where, n, send, recv, j):
-        at_line = (line + j) % LINE
+        at_line = place(j)
         piece_copy(where, n, send, recv, at_line, ten, (j, 0), ten).wait_recv()
         spread(where, n, send, recv, j)
 
     def att_copy(h, j, y, slot, to_seq, to_ten):
-        at_line, at_ten = (line + j) % LINE, pair_peer(y)
+        at_line, at_ten = place(j), pair_peer(y)
         at = att_at(h, at_line, at_ten)
         return remote(
             at, at, a_send.at[(h,) + slot], a_recv.at[h, at_line, at_ten], to_seq, to_ten
@@ -264,7 +280,7 @@
         sent.append(copy)
 
     def att_round(h, y):
-        for j in (2, 1, 3):
+        for j in (2, 1):
             att_send(h, 0, y, (j, y), line_peer(j), ten)
         att_send(h, 0, y, (0, pairs + y), seq, twin)
 
@@ -274,6 +290,8 @@
     scale = 1.0 / math.sqrt(HD)
     for h in range(2):
         kv_wait(h)
+        if h == 0:
+            guarded(holds, w_relay)
         block = seq if h == 0 else 2 * n_seq - 1 - seq
         query = jnp.concatenate(
             [q_ref[h * half : (h + 1) * half, g * HD : (g + 1) * HD] for g in range(heads)], axis=0
@@ -341,7 +359,7 @@
     cv_ref[...] = picked[:, HD:].astype(jnp.bfloat16)
 
     def multiply(u, j):
-        at_line = (line + j) % LINE
+        at_line = place(j)
 
         def add(k, total):
             return total + jnp.dot(
@@ -365,6 +383,33 @@
             copy.start()
             sent.append(copy)
 
+    square[...] = jnp.zeros_like(square)
+
+    def column(u, a, t):
+        place = ((t // parts * 2 + u) * LINE + a) * parts + t % parts
+        return pl.ds(pl.multiple_of(place * width, width), width)
+
+    def write(u, a, t):
+        return pltpu.make_async_copy(
+            proj.at[u, a, t], out_ref.at[:, column(u, a, t)], out_sem.at[u, a, t]
+        )
+
+    def collect(u, j):
+        settle(proj_at, u, p_send, p_recv, j)
+        at_line = place(j)
+
+        def add(t, carry):
+            write(u, at_line, t).start()
+            hidden = res[:, column(u, at_line, t)].astype(jnp.float32) + proj[
+                u, at_line, t
+            ].astype(jnp.float32)
+            power = hidden * hidden
+            for part in range(width // HD):
+                square[...] += power[:, part * HD : (part + 1) * HD]
+            return carry
+
+        lax.fori_loop(0, n_tensor, add, 0)
+
     order = (0, 2, 1, 3)
     other = 1 - slot
     w_wait(slot)
@@ -377,11 +422,14 @@
             for y in range(pairs):
                 if n > 0:
                     att_arrive(h, order[n], y)
+                    if order[n] == 2:
+                        att_send(h, 2, y, (3, y), line_peer(1), ten)
                     att_send(h, order[n], y, (order[n], pairs + y), seq, twin)
         for h in range(2):
             settle(att_at, h, a_send, a_recv, order[n])
         multiply(slot, order[n])
     w_wait(other)
+    res_copy.wait()
     for u, last in ((slot, False), (other, True)):
         for n in range(LINE):
             if not last:
@@ -389,37 +437,19 @@
             if n + 1 < LINE:
                 arrive(proj_at, u, p_send, p_recv, order[n + 1])
             relay(proj_at, u, p_send, p_recv, order[n])
-    res_copy.wait()
-    for u in (slot, other):
-        for n in range(LINE):
-            settle(proj_at, u, p_send, p_recv, order[n])
-
-    columns = res.shape[1]
-    places = [
-        (u, a, t, (((t // parts * 2 + u) * LINE + a) * parts + t % parts) * width)
-        for u in range(2)
-        for a in range(LINE)
-        for t in range(n_tensor)
-    ]
-
-    def finish(r, carry):
-        at = pl.ds(pl.multiple_of(r * ROW_TILE, ROW_TILE), ROW_TILE)
-        square = jnp.zeros((ROW_TILE, width), jnp.float32)
-        for u, a, t, lo in places:
-            hidden = res[at, lo : lo + width].astype(jnp.float32) + proj[u, a, t, at, :].astype(
-                jnp.float32
-            )
-            square = square + hidden * hidden
-        factor = lax.rsqrt(jnp.sum(square, axis=1, keepdims=True) * (1.0 / columns) + 1e-05)
-        for u, a, t, lo in places:
-            hidden = res[at, lo : lo + width].astype(jnp.float32) + proj[u, a, t, at, :].astype(
-                jnp.float32
-            )
-            gain = gain_ref[:, lo : lo + width].astype(jnp.float32)
-            normed_ref[at, lo : lo + width] = (hidden * factor * gain).astype(jnp.bfloat16)
-        return carry
-
-    lax.fori_loop(0, rows // ROW_TILE, finish, 0)
+            if not last and n > 0:
+                collect(u, order[n - 1])
+            if last and n == 0:
+                collect(slot, order[LINE - 1])
+    for n in range(LINE):
+        collect(other, order[n])
+    total = jnp.sum(square[...], axis=1, keepdims=True)
+    factor = lax.rsqrt(total * (1.0 / res.shape[1]) + 1e-05)
+    factor_ref[...] = jnp.broadcast_to(factor, factor_ref.shape)
+    for u in range(2):
+        for a in range(LINE):
+            for t in range(n_tensor):
+                write(u, a, t).wait()
 
     for copy in sent:
         copy.wait_send()
@@ -449,15 +479,16 @@
     vmem = pl.BlockSpec(memory_space=pltpu.VMEM)
     hbm = pl.BlockSpec(memory_space=pl.ANY)
     dma = pltpu.SemaphoreType.DMA
-    return pl.pallas_call(
+    projected, factor, cache_keys, cache_values = pl.pallas_call(
         functools.partial(kernel, n_seq, n_tensor),
         out_shape=(
             jax.ShapeDtypeStruct((rows, model), jnp.bfloat16),
+            jax.ShapeDtypeStruct((rows, HD), jnp.float32),
             jax.ShapeDtypeStruct((SLOT_DEV, HD), jnp.bfloat16),
             jax.ShapeDtypeStruct((SLOT_DEV, HD), jnp.bfloat16),
         ),
-        in_specs=[vmem, vmem, vmem, hbm, hbm, vmem, pl.BlockSpec(memory_space=pltpu.SMEM)],
-        out_specs=(vmem, vmem, vmem),
+        in_specs=[vmem, vmem, vmem, hbm, hbm, pl.BlockSpec(memory_space=pltpu.SMEM)],
+        out_specs=(hbm, vmem, vmem, vmem),
         scratch_shapes=[
             pltpu.VMEM((rows * n_seq, 2 * HD), jnp.bfloat16),
             pltpu.VMEM((2, n_tensor, depth, width), jnp.bfloat16),
@@ -468,6 +499,7 @@
             pltpu.VMEM((stack, HD), jnp.float32),
             pltpu.VMEM((stack, HD), jnp.float32),
             pltpu.VMEM((stack, HD), jnp.float32),
+            pltpu.VMEM((rows, HD), jnp.float32),
             dma((rest, LINE, 2)),
             dma((n_seq, 2)),
             dma((parts,)),
@@ -480,6 +512,7 @@
             dma((2, LINE, 2 * pairs)),
             dma((2, LINE, n_tensor)),
             dma,
+            dma((2, LINE, n_tensor)),
         ],
         compiler_params=pltpu.CompilerParams(
             collective_id=0, has_side_effects=True, vmem_limit_bytes=58 * 2**20
@@ -493,9 +526,11 @@
         value_rows,
         out_weight,
         residual_in,
-        norm_gain.reshape(1, model),
         lengths,
     )
+    hidden = residual_in.astype(jnp.float32) + projected.astype(jnp.float32)
+    normed = hidden * factor[:, :1] * norm_gain.astype(jnp.float32)
+    return normed.astype(jnp.bfloat16), cache_keys, cache_values
 
 
 def solution(mesh):

time: 134 us -> 140 us (1.045)
  other arithmetic: 0 us -> 8.05 us
  local copies, waits for them, and re-layouts: 8.18 us -> 2.41 us
  Pallas kernels: 124 us -> 128 us
    convert_element_type x0 -> x2, other arithmetic: none -> 8.05 us  [the longest x1 7.33 us: body(): return (normed.astype(jnp.bfloat16), cache_keys, cache_values)]
    unnamed x7 -> x8, local copies, waits for them, and re-layouts: 6.83 us -> 1.36 us
    pallas_call x1, Pallas kernels: 124 us -> 128 us  [body(): pl.pallas_call(functools.partial(kernel, n_seq, n_tensor), out_shape=(jax...]
where the time goes in v4:
time: 140 us; the launch traced here: 139 us
  Pallas kernels  128 us (91%)
  other arithmetic  8.05 us (6%)
  local copies, waits for them, and re-layouts  2.41 us (2%)
    pallas_call x1, Pallas kernels, body(): pl.pallas_call(functools.partial(kernel, n_seq, n_tensor), out_shape=(jax...  128 us
    convert_element_type x1, other arithmetic, body(): return (normed.astype(jnp.bfloat16), cache_keys, cache_values)  7.33 us

profile of v4, /device:TPU:0, one launch (start us, length us, event | category | flops | bytes accessed | tf_op | source)
XLA Modules:
  0.0 139.4 jit_solution(15972355678038973125)
XLA Ops:
  0.6 0.7 convert_element_type.14
  1.4 0.0 copy-start
  1.4 128.3 %shard_map.94 = (bf16[320,8192]{1,0:T(8,128)(2,1)}, f32[320,128]{1,0:T(8,128)}, bf16[704,128]{1,0:T(8,128)(2,1)}, bf16[704,128]{1,0:T(8,128)(2,1)}) custom-call(bf16[320,512]{1,0:T(8,128)(2,1)} %q_ref.1, bf16[320,128]{1,0:T(8,128)(2,1)} %k_ref.1, bf16[320,128]{1,0:T(8,128)(2,1)} %v_ref.1, bf16[512,1024]{1,0:T(8,128)(2,1)} %w_ref.1, ...), custom_call_target="tpu_custom_call" | custom-call | flops 5000000000 | bytes 14000000 | tf_op jit(solution)/shard_map/pallas_call | solution.py:482
  129.6 1.1 slice_reduce_fusion
  130.7 0.0 copy-done
  130.7 0.0 copy-start.2
  130.7 0.0 copy-start.1
  130.7 7.3 %multiply_convert_fusion = bf16[320,8192]{1,0:T(8,128)(2,1)} fusion(bf16[320,8192]{1,0:T(8,128)(2,1)} %get-tuple-element.7, bf16[320,8192]{1,0:T(8,128)(2,1)S(1)} %copy-done, f32[8192]{0:T(1024)S(1)} %convert_element_type.14, f32[320]{0:T(512)S(1)} %slice_reduce_fusion), kind=kLoop, calls=%fused_computation | loop fusion | flops 15728640 | bytes 15762688 | tf_op jit(solution)/shard_map/convert_element_type | solution.py:533
  138.0 0.0 copy-done.2
  138.0 0.7 copy.12
  138.7 0.0 copy-done.1
  138.7 0.7 copy.13
Async XLA Ops:
  1.4 129.3 %copy-start = (bf16[320,8192]{1,0:T(8,128)(2,1)S(1)}, bf16[320,8192]{1,0:T(8,128)(2,1)}, u32[]{:S(2)}) copy-start(bf16[320,8192]{1,0:T(8,128)(2,1)} %res_ref.1) | copy-start | bytes 15728644
  130.7 7.3 %copy-start.2 = (bf16[704,128]{1,0:T(8,128)(2,1)S(1)}, bf16[704,128]{1,0:T(8,128)(2,1)}, u32[]{:S(2)}) copy-start(bf16[704,128]{1,0:T(8,128)(2,1)} %get-tuple-element.15) | copy-start | bytes 540676
  130.7 8.0 %copy-start.1 = (bf16[704,128]{1,0:T(8,128)(2,1)S(1)}, bf16[704,128]{1,0:T(8,128)(2,1)}, u32[]{:S(2)}) copy-start(bf16[704,128]{1,0:T(8,128)(2,1)} %get-tuple-element.16) | copy-start | bytes 540676

commit v5 on v4

--- a/solution.py
+++ b/solution.py
@@ -173,6 +173,7 @@
         )
 
     def w_begin():
+        w_keep().start()
         for i in range(1, rest):
             w_second(i, 0).start()
 
@@ -180,7 +181,7 @@
         pl.when(jnp.logical_not(holds))(lambda: w_first(0).start())
     for k in range(1, parts):
         w_first(k).start()
-    guarded(holds, lambda: w_keep().start())
+    guarded(holds, w_begin)
 
     def kv_arrive(i, j, h):
         kv_copy(kv_source(i, j), h, i, j, seq).wait_recv()
@@ -199,7 +200,6 @@
             kv_relay(i, h)
 
     def w_relay():
-        w_begin()
         for k in range(1, n_tensor):
             source = (ten + k) % n_tensor
             remote(
@@ -208,6 +208,8 @@
             for i in range(1, rest):
                 w_second(i, k).start()
         w_keep().wait()
+
+    guarded(holds, w_relay)
 
     def w_wait(u):
         owner = ten // parts * 2 + u
@@ -287,15 +289,10 @@
     def att_arrive(h, j, y):
         att_copy(h, j, y, (0, 0), seq, ten).wait_recv()
 
-    scale = 1.0 / math.sqrt(HD)
+    scale = math.log2(math.e) / math.sqrt(HD)
     for h in range(2):
         kv_wait(h)
-        if h == 0:
-            guarded(holds, w_relay)
         block = seq if h == 0 else 2 * n_seq - 1 - seq
-        query = jnp.concatenate(
-            [q_ref[h * half : (h + 1) * half, g * HD : (g + 1) * HD] for g in range(heads)], axis=0
-        )
         position = block * half + lax.broadcasted_iota(jnp.int32, (half, 1), 0)
         begin = jnp.zeros((half, 1), jnp.int32)
         for p in range(1, n_prompts):
@@ -304,59 +301,37 @@
         l_ref[...] = jnp.zeros_like(l_ref)
         acc_ref[...] = jnp.zeros_like(acc_ref)
 
-        def step(c, carry, query=query, position=position, begin=begin):
+        def step(c, carry, h=h, position=position, begin=begin):
             at = pl.ds(pl.multiple_of(c * KEYS, KEYS), KEYS)
-            scores = lax.dot_general(
-                query,
-                kv[at, :HD],
-                (((1,), (1,)), ((), ())),
-                preferred_element_type=jnp.float32,
-            )
             where = c * KEYS + lax.broadcasted_iota(jnp.int32, (half, KEYS), 1)
             bias = jnp.where((where >= begin) & (where <= position), 0.0, -1e30)
-            scores = scores * scale + jnp.concatenate([bias] * heads, axis=0)
-            old = m_ref[:, :1]
-            top = jnp.maximum(old, jnp.max(scores, axis=1, keepdims=True))
-            shrink = jnp.exp(old - top)
-            weights = jnp.exp(scores - top)
-            total = l_ref[:, :1] * shrink + jnp.sum(weights, axis=1, keepdims=True)
-            acc_ref[...] = acc_ref[...] * shrink + jnp.dot(
-                weights.astype(jnp.bfloat16), kv[at, HD:], preferred_element_type=jnp.float32
-            )
-            m_ref[...] = jnp.broadcast_to(top, m_ref.shape)
-            l_ref[...] = jnp.broadcast_to(total, l_ref.shape)
+            for g in range(heads):
+                scores = lax.dot_general(
+                    q_ref[h * half : (h + 1) * half, g * HD : (g + 1) * HD],
+                    kv[at, :HD],
+                    (((1,), (1,)), ((), ())),
+                    preferred_element_type=jnp.float32,
+                )
+                scores = scores * scale + bias
+                old = m_ref[g]
+                top = jnp.maximum(old, jnp.max(scores, axis=1, keepdims=True))
+                shrink = jnp.exp2(old - top)
+                weights = jnp.exp2(scores - jnp.concatenate([top] * (KEYS // HD), axis=1))
+                l_ref[g] = l_ref[g] * shrink + jnp.sum(weights, axis=1, keepdims=True)
+                acc_ref[g] = acc_ref[g] * shrink + jnp.dot(
+                    weights.astype(jnp.bfloat16), kv[at, HD:], preferred_element_type=jnp.float32
+                )
+                m_ref[g] = top
             return carry
 
         lax.fori_loop(0, ((block + 1) * half + KEYS - 1) // KEYS, step, 0)
-        result = (acc_ref[...] / l_ref[...]).astype(jnp.bfloat16)
         for g in range(heads):
-            att[line, ten, h * half : (h + 1) * half, g * HD : (g + 1) * HD] = result[
-                g * half : (g + 1) * half
-            ]
+            att[line, ten, h * half : (h + 1) * half, g * HD : (g + 1) * HD] = (
+                acc_ref[g] / l_ref[g]
+            ).astype(jnp.bfloat16)
         for i in range(1, pairs):
             att_send(h, 0, 0, (0, i), seq, pair_peer(i))
         att_round(h, 0)
-
-    slots = seq * SLOT_DEV + lax.broadcasted_iota(jnp.int32, (SLOT_DEV, 1), 0)
-    source_of = jnp.full((SLOT_DEV, 1), -1, jnp.int32)
-    page = jnp.int32(0)
-    for p in range(n_prompts):
-        length = len_ref[p]
-        within = slots - page
-        live = (within >= 0) & (within < length)
-        source_of = jnp.where(live, within + starts[p], source_of)
-        page = page + (length + PAGE - 1) // PAGE * PAGE
-    picked = jnp.zeros((SLOT_DEV, 2 * HD), jnp.float32)
-
-    def pick(c, picked):
-        at = pl.ds(pl.multiple_of(c * KEYS, KEYS), KEYS)
-        where = c * KEYS + lax.broadcasted_iota(jnp.int32, (SLOT_DEV, KEYS), 1)
-        hot = jnp.where(where == source_of, 1.0, 0.0).astype(jnp.bfloat16)
-        return picked + jnp.dot(hot, kv[at, :], preferred_element_type=jnp.float32)
-
-    picked = lax.fori_loop(0, tokens // KEYS, pick, picked)
-    ck_ref[...] = picked[:, :HD].astype(jnp.bfloat16)
-    cv_ref[...] = picked[:, HD:].astype(jnp.bfloat16)
 
     def multiply(u, j):
         at_line = place(j)
@@ -428,6 +403,27 @@
         for h in range(2):
             settle(att_at, h, a_send, a_recv, order[n])
         multiply(slot, order[n])
+    slots = seq * SLOT_DEV + lax.broadcasted_iota(jnp.int32, (SLOT_DEV, 1), 0)
+    source_of = jnp.full((SLOT_DEV, 1), -1, jnp.int32)
+    page = jnp.int32(0)
+    for p in range(n_prompts):
+        length = len_ref[p]
+        within = slots - page
+        live = (within >= 0) & (within < length)
+        source_of = jnp.where(live, within + starts[p], source_of)
+        page = page + (length + PAGE - 1) // PAGE * PAGE
+    picked = jnp.zeros((SLOT_DEV, 2 * HD), jnp.float32)
+
+    def pick(c, picked):
+        at = pl.ds(pl.multiple_of(c * KEYS, KEYS), KEYS)
+        where = c * KEYS + lax.broadcasted_iota(jnp.int32, (SLOT_DEV, KEYS), 1)
+        hot = jnp.where(where == source_of, 1.0, 0.0).astype(jnp.bfloat16)
+        return picked + jnp.dot(hot, kv[at, :], preferred_element_type=jnp.float32)
+
+    picked = lax.fori_loop(0, tokens // KEYS, pick, picked)
+    ck_ref[...] = picked[:, :HD].astype(jnp.bfloat16)
+    cv_ref[...] = picked[:, HD:].astype(jnp.bfloat16)
+
     w_wait(other)
     res_copy.wait()
     for u, last in ((slot, False), (other, True)):
@@ -474,7 +470,7 @@
     rest, pairs = n_seq // LINE, n_tensor // CORES
     parts = out_weight.shape[1] // width
     half = rows // 2
-    stack = queries.shape[1] // HD * half
+    heads = queries.shape[1] // HD
     depth = out_weight.shape[0]
     vmem = pl.BlockSpec(memory_space=pltpu.VMEM)
     hbm = pl.BlockSpec(memory_space=pl.ANY)
@@ -496,9 +492,9 @@
             pltpu.VMEM((2, LINE, rows, width), jnp.bfloat16),
             pltpu.VMEM((2, LINE, n_tensor, rows, width), jnp.bfloat16),
             pltpu.VMEM((rows, model), jnp.bfloat16),
-            pltpu.VMEM((stack, HD), jnp.float32),
-            pltpu.VMEM((stack, HD), jnp.float32),
-            pltpu.VMEM((stack, HD), jnp.float32),
+            pltpu.VMEM((heads, half, HD), jnp.float32),
+            pltpu.VMEM((heads, half, HD), jnp.float32),
+            pltpu.VMEM((heads, half, HD), jnp.float32),
             pltpu.VMEM((rows, HD), jnp.float32),
             dma((rest, LINE, 2)),
             dma((n_seq, 2)),

time: 140 us -> 129 us (0.921)
  Pallas kernels: 128 us -> 117 us
    pallas_call x1, Pallas kernels: 128 us -> 117 us  [body(): pl.pallas_call(functools.partial(kernel, n_seq, n_tensor), out_shape=(jax...]
where the time goes in v5:
time: 129 us; the launch traced here: 128 us
  Pallas kernels  117 us (91%)
  other arithmetic  8.05 us (6%)
  local copies, waits for them, and re-layouts  2.41 us (2%)
    pallas_call x1, Pallas kernels, body(): pl.pallas_call(functools.partial(kernel, n_seq, n_tensor), out_shape=(jax...  117 us
    convert_element_type x1, other arithmetic, body(): return (normed.astype(jnp.bfloat16), cache_keys, cache_values)  7.33 us

profile of v5, /device:TPU:0, one launch (start us, length us, event | category | flops | bytes accessed | tf_op | source)
XLA Modules:
  0.0 128.4 jit_solution(13015583395164605281)
XLA Ops:
  0.6 0.7 convert_element_type.14
  1.4 0.0 copy-start
  1.4 117.3 %shard_map.94 = (bf16[320,8192]{1,0:T(8,128)(2,1)}, f32[320,128]{1,0:T(8,128)}, bf16[704,128]{1,0:T(8,128)(2,1)}, bf16[704,128]{1,0:T(8,128)(2,1)}) custom-call(bf16[320,512]{1,0:T(8,128)(2,1)} %q_ref.1, bf16[320,128]{1,0:T(8,128)(2,1)} %k_ref.1, bf16[320,128]{1,0:T(8,128)(2,1)} %v_ref.1, bf16[512,1024]{1,0:T(8,128)(2,1)} %w_ref.1, ...), custom_call_target="tpu_custom_call" | custom-call | flops 5000000000 | bytes 14000000 | tf_op jit(solution)/shard_map/pallas_call | solution.py:478
  118.7 1.1 slice_reduce_fusion
  119.7 0.0 copy-done
  119.7 0.0 copy-start.2
  119.8 0.0 copy-start.1
  119.8 7.3 %multiply_convert_fusion = bf16[320,8192]{1,0:T(8,128)(2,1)} fusion(bf16[320,8192]{1,0:T(8,128)(2,1)} %get-tuple-element.7, bf16[320,8192]{1,0:T(8,128)(2,1)S(1)} %copy-done, f32[8192]{0:T(1024)S(1)} %convert_element_type.14, f32[320]{0:T(512)S(1)} %slice_reduce_fusion), kind=kLoop, calls=%fused_computation | loop fusion | flops 15728640 | bytes 15762688 | tf_op jit(solution)/shard_map/convert_element_type | solution.py:529
  127.1 0.0 copy-done.2
  127.1 0.7 copy.12
  127.8 0.0 copy-done.1
  127.8 0.7 copy.13
Async XLA Ops:
  1.4 118.4 %copy-start = (bf16[320,8192]{1,0:T(8,128)(2,1)S(1)}, bf16[320,8192]{1,0:T(8,128)(2,1)}, u32[]{:S(2)}) copy-start(bf16[320,8192]{1,0:T(8,128)(2,1)} %res_ref.1) | copy-start | bytes 15728644
  119.7 7.3 %copy-start.2 = (bf16[704,128]{1,0:T(8,128)(2,1)S(1)}, bf16[704,128]{1,0:T(8,128)(2,1)}, u32[]{:S(2)}) copy-start(bf16[704,128]{1,0:T(8,128)(2,1)} %get-tuple-element.15) | copy-start | bytes 540676
  119.8 8.0 %copy-start.1 = (bf16[704,128]{1,0:T(8,128)(2,1)S(1)}, bf16[704,128]{1,0:T(8,128)(2,1)}, u32[]{:S(2)}) copy-start(bf16[704,128]{1,0:T(8,128)(2,1)} %get-tuple-element.16) | copy-start | bytes 540676

commit v6 on v5

--- a/solution.py
+++ b/solution.py
@@ -403,6 +403,9 @@
         for h in range(2):
             settle(att_at, h, a_send, a_recv, order[n])
         multiply(slot, order[n])
+    for n in range(1, LINE):
+        arrive(proj_at, slot, p_send, p_recv, order[n])
+
     slots = seq * SLOT_DEV + lax.broadcasted_iota(jnp.int32, (SLOT_DEV, 1), 0)
     source_of = jnp.full((SLOT_DEV, 1), -1, jnp.int32)
     page = jnp.int32(0)
@@ -426,17 +429,15 @@
 
     w_wait(other)
     res_copy.wait()
-    for u, last in ((slot, False), (other, True)):
-        for n in range(LINE):
-            if not last:
-                multiply(other, order[n])
-            if n + 1 < LINE:
-                arrive(proj_at, u, p_send, p_recv, order[n + 1])
-            relay(proj_at, u, p_send, p_recv, order[n])
-            if not last and n > 0:
-                collect(u, order[n - 1])
-            if last and n == 0:
-                collect(slot, order[LINE - 1])
+    for n in range(LINE):
+        multiply(other, order[n])
+    for n in range(LINE):
+        if n + 1 < LINE:
+            arrive(proj_at, other, p_send, p_recv, order[n + 1])
+        relay(proj_at, slot, p_send, p_recv, order[n])
+    for n in range(LINE):
+        collect(slot, order[n])
+        relay(proj_at, other, p_send, p_recv, order[n])
     for n in range(LINE):
         collect(other, order[n])
     total = jnp.sum(square[...], axis=1, keepdims=True)

time: 129 us -> 125 us (0.969)
  Pallas kernels: 117 us -> 114 us
    pallas_call x1, Pallas kernels: 117 us -> 114 us  [body(): pl.pallas_call(functools.partial(kernel, n_seq, n_tensor), out_shape=(jax...]
where the time goes in v6:
time: 125 us
  Pallas kernels  114 us (91%)
  other arithmetic  8.05 us (6%)
  local copies, waits for them, and re-layouts  2.41 us (2%)
    pallas_call x1, Pallas kernels, body(): pl.pallas_call(functools.partial(kernel, n_seq, n_tensor), out_shape=(jax...  114 us
    convert_element_type x1, other arithmetic, body(): return (normed.astype(jnp.bfloat16), cache_keys, cache_values)  7.33 us

profile of v6, /device:TPU:0, one launch (start us, length us, event | category | flops | bytes accessed | tf_op | source)
XLA Modules:
  0.0 124.6 jit_solution(8917695080175375885)
XLA Ops:
  0.6 0.7 convert_element_type.14
  1.4 0.0 copy-start
  1.4 113.5 %shard_map.94 = (bf16[320,8192]{1,0:T(8,128)(2,1)}, f32[320,128]{1,0:T(8,128)}, bf16[704,128]{1,0:T(8,128)(2,1)}, bf16[704,128]{1,0:T(8,128)(2,1)}) custom-call(bf16[320,512]{1,0:T(8,128)(2,1)} %q_ref.1, bf16[320,128]{1,0:T(8,128)(2,1)} %k_ref.1, bf16[320,128]{1,0:T(8,128)(2,1)} %v_ref.1, bf16[512,1024]{1,0:T(8,128)(2,1)} %w_ref.1, ...), custom_call_target="tpu_custom_call" | custom-call | flops 5000000000 | bytes 14000000 | tf_op jit(solution)/shard_map/pallas_call | solution.py:479
  114.9 1.1 slice_reduce_fusion
  115.9 0.0 copy-done
  115.9 0.0 copy-start.2
  115.9 0.0 copy-start.1
  116.0 7.3 %multiply_convert_fusion = bf16[320,8192]{1,0:T(8,128)(2,1)} fusion(bf16[320,8192]{1,0:T(8,128)(2,1)} %get-tuple-element.7, bf16[320,8192]{1,0:T(8,128)(2,1)S(1)} %copy-done, f32[8192]{0:T(1024)S(1)} %convert_element_type.14, f32[320]{0:T(512)S(1)} %slice_reduce_fusion), kind=kLoop, calls=%fused_computation | loop fusion | flops 15728640 | bytes 15762688 | tf_op jit(solution)/shard_map/convert_element_type | solution.py:530
  123.3 0.0 copy-done.2
  123.3 0.7 copy.12
  124.0 0.0 copy-done.1
  124.0 0.7 copy.13
Async XLA Ops:
  1.4 114.6 %copy-start = (bf16[320,8192]{1,0:T(8,128)(2,1)S(1)}, bf16[320,8192]{1,0:T(8,128)(2,1)}, u32[]{:S(2)}) copy-start(bf16[320,8192]{1,0:T(8,128)(2,1)} %res_ref.1) | copy-start | bytes 15728644
  115.9 7.3 %copy-start.2 = (bf16[704,128]{1,0:T(8,128)(2,1)S(1)}, bf16[704,128]{1,0:T(8,128)(2,1)}, u32[]{:S(2)}) copy-start(bf16[704,128]{1,0:T(8,128)(2,1)} %get-tuple-element.15) | copy-start | bytes 540676
  115.9 8.0 %copy-start.1 = (bf16[704,128]{1,0:T(8,128)(2,1)S(1)}, bf16[704,128]{1,0:T(8,128)(2,1)}, u32[]{:S(2)}) copy-start(bf16[704,128]{1,0:T(8,128)(2,1)} %get-tuple-element.16) | copy-start | bytes 540676
